TPU v7x, 256 devices: a whole 4x4x8 slice. The times are simulated.
256 devices in a mesh: order: 8 (over z_lo, core), lat: 32 (over y, x, z_hi).
Axes of the slice: x: 4, y: 4, z: 8 (z_hi: 2, z_lo: 4; z = z_hi * 4 + z_lo), core: 2. Of those that a mesh axis runs over, the one named last changes fastest.
Arguments:
- control: float32 [2, 3, 2, 1280, 1280], P(None, None, None, ('order', 'lat')), may hold values from -6 to 6
- vertical: float32 [3, 2, 2, 1280], replicated, may hold values from -4 to 4
- legendre: bfloat16 [1280, 1280, 640], P(('order', 'lat')), may hold values from -0.0034179688 to 0.0034179688
- order_assign: int32 [1280], replicated, may hold values from 0 to 1279, each once
- send_list: int32 [8, 32, 256], P('order', 'lat'), may hold values from 0 to 199
- used_slot_counts: int32 [8, 32, 32], P('order', 'lat'), may hold values from 1 to 8, as said below
- obs_count: int32 [8, 32, 256], P('order', 'lat'), may hold values from 1 to 16
- obs_var: int32 [8, 32, 4096], P('order', 'lat'), may hold values from 0 to 5
- obs_col: int32 [8, 32, 4096], P('order', 'lat'), may hold values from 0 to 60
- obs_weight: float32 [4, 8, 32, 4096], P(None, 'order', 'lat'), may hold values from 0.1 to 0.9
- obs_value: float32 [8, 32, 4096], P('order', 'lat'), may hold values from -6 to 6
- obs_error: float32 [8, 32, 4096], P('order', 'lat'), may hold values from 0.1 to 1
Outputs:
- increment: bfloat16 [1280, 6, 2560], P(('order', 'lat'))
- weighted: float32 [8, 32, 4096], P('order', 'lat')
- gradient: float32 [2, 3, 2, 1280, 1280], P(None, None, None, ('order', 'lat'))
Inputs may be any that keep to these rules, and one draw needn't show every extreme that they name: `send_list`: entries for slots t >= used_slot_counts[o, d, s] are not read. `used_slot_counts`: in every order group one owner receives 8 blocks from every source device. `order_assign`: each order once.
All inputs are finite; a program needn't handle non-finite values.
Results may differ from a plain program's by a relative error of at most 0.0062.
Values may be sent and summed in bfloat16 or wider, within the bound.
No kernel may reach another device: no remote copies, remote signals or barrier semaphores. Data moves between devices by JAX's collectives and lax.ppermute only.
A program may use at most 128 MiB of HBM per device.

v0:
```python
import functools
import math

import jax
import jax.numpy as jnp
from jax import lax
from jax.experimental import pallas as pl
from jax.experimental.pallas import tpu as pltpu
from jax.sharding import PartitionSpec as P

NLON = 2560
QUARTER = NLON // 4
BLKW = 64
CAP = 8
KOBS = 16
MM = 1280
NHALF = 640
VARS = 6
ROWS = 5
ORDERS = 5
DEVS = 256
N_LAT = 32
CHUNKS = NLON // 128
F32 = jnp.float32
BF16 = jnp.bfloat16
NT = (((1,), (1,)), ((), ()))


def lanes(shape, axis):
    return lax.broadcasted_iota(jnp.int32, shape, axis)


def pack_obs(var_ref, col_ref, weight_ref, value_ref, error_ref, used_ref, count_ref, out_ref):
    source = lanes((N_LAT, DEVS), 0)
    slot = lanes((N_LAT, DEVS), 1)
    mine = jnp.where(slot // CAP == source, count_ref[...].astype(F32), 0.0).astype(BF16)
    spread = (lanes((DEVS, 128), 0) % CAP == lanes((DEVS, 128), 1) // KOBS).astype(F32).astype(BF16)
    counts = jnp.dot(mine, spread, preferred_element_type=F32)
    own = lanes((N_LAT, N_LAT), 0) == lanes((N_LAT, N_LAT), 1)
    used = jnp.sum(jnp.where(own, used_ref[...].astype(F32), 0.0), axis=1, keepdims=True)
    lane = lanes((N_LAT, 128), 1)
    live = ((lane // KOBS).astype(F32) < used) & ((lane % KOBS).astype(F32) < counts)
    fields = [weight_ref[w] for w in range(4)]
    fields.append(var_ref[...].astype(F32))
    fields.append(col_ref[...].astype(F32))
    fields.append(value_ref[...])
    fields.append(jnp.where(live, 1.0 / error_ref[...], 0.0))
    for index, field in enumerate(fields):
        out_ref[pl.ds(index, N_LAT, stride=8), :] = field


def row_picks(half, row):
    device = lanes((128, NHALF), 0)
    at = lanes((128, NHALF), 1)
    want = device * ROWS + row if half == 0 else (NHALF - 1 - row) - device * ROWS
    return jnp.where(at == want, 1.0, 0.0).astype(BF16)


def start_tables(legendre_ref, table_ref, sems):
    copies = [
        pltpu.make_async_copy(legendre_ref.at[i], table_ref.at[i], sems.at[i]) for i in range(ORDERS)
    ]
    for copy in copies:
        copy.start()
    return copies


def alternate_signs():
    return jnp.where(lanes((1, MM), 1) % 2 == 0, 1.0, -1.0)


def synth_kernel(
    order_ref, vertical_ref, control_ref, legendre_ref, out_ref, lookup_ref, table_ref, padded_ref, mixed_ref, half_ref, rows_ref, sems
):
    copies = start_tables(legendre_ref, table_ref, sems)
    first = (lax.axis_index("order") * N_LAT + lax.axis_index("lat")) * ORDERS
    padded_ref[...] = jnp.zeros_like(padded_ref)
    for f in range(3):
        for a in range(2):
            padded_ref[pl.ds(f * 4 + a * 2, 2), pl.ds(0, MM)] = vertical_ref[f, a]
    for i in range(ORDERS):
        order = order_ref[first + i]
        base = pl.multiple_of((order // 128) * 128, 128)
        window = padded_ref[:, pl.ds(base, MM + 128)]
        window = pltpu.roll(window, (MM + 128) - order % 128, 1)
        for u in range(MM // 128):
            lookup_ref[u, pl.ds(i, 12, stride=8), :] = window[:12, 128 * u : 128 * u + 128]
    for c in range(2):
        for f in range(3):
            for a in range(2):
                for u in range(MM // 128):
                    at = pl.ds(128 * u, 128)
                    mix = lookup_ref[u, pl.ds((f * 4 + a * 2) * 8, ORDERS), :] * control_ref[c * 6 + f * 2, :, at]
                    other = lookup_ref[u, pl.ds((f * 4 + a * 2 + 1) * 8, ORDERS), :]
                    mix = mix + other * control_ref[c * 6 + f * 2 + 1, :, at]
                    mixed_ref[u, pl.ds((c * 6 + f * 2 + a) * 8, ORDERS), :] = mix
    signs = alternate_signs()
    half_ref[...] = jnp.zeros_like(half_ref)
    for i in range(ORDERS):
        coeffs = jnp.concatenate([mixed_ref[u, pl.ds(i, 12, stride=8), :] for u in range(MM // 128)], axis=1)
        signed = jnp.concatenate([coeffs, coeffs * signs], axis=0).astype(BF16)
        copies[i].wait()
        both = jnp.dot(signed, table_ref[i], preferred_element_type=F32)
        half_ref[0, pl.ds(12 * i, 12), :] = both[:12]
        half_ref[1, pl.ds(12 * i, 12), :] = both[12:]
    low = lanes((128, 128), 1) < 64
    for half in range(2):
        rows = half_ref[half].astype(BF16)
        rows = jnp.concatenate([rows, rows], axis=0)
        picked = [
            lax.dot_general(row_picks(half, j), rows, NT, preferred_element_type=F32) for j in range(ROWS)
        ]
        picked.append(jnp.zeros_like(picked[0]))
        for jj in range(3):
            rows_ref[pl.ds(half * 512 + jj, 128, stride=4), :] = jnp.where(low, picked[2 * jj], picked[2 * jj + 1])
        rows_ref[pl.ds(half * 512 + 3, 128, stride=4), :] = jnp.zeros((128, 128), F32)
    out_ref[...] = rows_ref[...].astype(BF16)


def turn(steps):
    quadrant = jnp.floor(steps * (1.0 / QUARTER) + 0.5)
    angle = (steps - quadrant * QUARTER) * (2.0 * math.pi / NLON)
    square = angle * angle
    sine = angle * (
        1.0 + square * (-1.0 / 6 + square * (1.0 / 120 + square * (-1.0 / 5040 + square * (1.0 / 362880))))
    )
    cosine = 1.0 + square * (
        -0.5 + square * (1.0 / 24 + square * (-1.0 / 720 + square * (1.0 / 40320 - square * (1.0 / 3628800))))
    )
    part = quadrant - 4.0 * jnp.floor(quadrant * 0.25)
    odd = (part == 1.0) | (part == 3.0)
    cos_sign = jnp.where((part == 1.0) | (part == 2.0), -1.0, 1.0)
    sin_sign = jnp.where(part >= 2.0, -1.0, 1.0)
    return cos_sign * jnp.where(odd, sine, cosine), sin_sign * jnp.where(odd, cosine, sine)


def phase_kernel(order_ref, out_ref):
    lane = lanes((DEVS, 128), 1).astype(F32)
    for i in range(ORDERS):
        order = order_ref[:, i : i + 1].astype(F32)
        weight = jnp.where(order == 0.0, 1.0, 2.0)
        fine_cos, fine_sin = turn(order * lane)
        fine_cos, fine_sin = fine_cos * weight, fine_sin * weight
        for a in range(QUARTER // 128):
            big_cos, big_sin = turn(order * (128.0 * a))
            out_ref[pl.ds(i * DEVS, DEVS), pl.ds(128 * a, 128)] = (fine_cos * big_cos - fine_sin * big_sin).astype(BF16)
            out_ref[pl.ds((ORDERS + i) * DEVS, DEVS), pl.ds(128 * a, 128)] = (
                -(fine_sin * big_cos + fine_cos * big_sin)
            ).astype(BF16)


def class_masks(order_row):
    residue = order_row % 4
    zero = jnp.where(residue == 0, 1.0, 0.0)
    two = jnp.where(residue == 2, 1.0, 0.0)
    odd = jnp.where(residue % 2 == 1, 1.0, 0.0)
    turned = jnp.where(residue == 1, 1.0, jnp.where(residue == 3, -1.0, 0.0))
    return zero, two, odd, turned


def middle_kernel(
    send_smem, send_ref, order_ref, obs_ref, rows_ref, phase_ref, inc_ref, out_ref,
    wide_ref, turned_ref, grouped_ref, lhs_ref, grid_ref, acc_ref, seen_ref,
):
    wide_ref[...] = rows_ref[...].astype(F32)
    for jj in range(3):
        turned_ref[pl.ds(128 * jj, 128), :] = wide_ref[pl.ds(jj, DEVS, stride=4), :].T
    grouped_ref[...] = jnp.zeros_like(grouped_ref)
    for g in range(2 * ORDERS):
        for j in range(ROWS):
            grouped_ref[g, pl.ds(6 * j, 6), :] = turned_ref[pl.ds(64 * j + 6 * g, 6), :]
    masks = [class_masks(order_ref[i : i + 1, :]) for i in range(ORDERS)]
    for i in range(ORDERS):
        zero, two, odd, turned = masks[i]
        real, imag = grouped_ref[2 * i], grouped_ref[2 * i + 1]
        by_cos = jnp.concatenate([real * zero, real * two, real * odd, imag * turned], axis=0)
        by_sin = jnp.concatenate([imag * zero, imag * two, imag * odd, -(real * turned)], axis=0)
        lhs_ref[:, pl.ds(i * DEVS, DEVS)] = by_cos.astype(BF16)
        lhs_ref[:, pl.ds((ORDERS + i) * DEVS, DEVS)] = by_sin.astype(BF16)
    sums = jnp.dot(lhs_ref[...], phase_ref[...], preferred_element_type=F32)
    r0, r2, ro, io = (sums[32 * k : 32 * k + 32] for k in range(4))
    even, skew = r0 + r2, r0 - r2
    quarters = [even + ro, skew - io, even - ro, skew + io]
    for a in range(4):
        rounded = quarters[a].astype(BF16).astype(F32)
        for u in range(5):
            grid_ref[a * 5 + u] = rounded[:, 128 * u : 128 * u + 128]
        for j in range(ROWS):
            inc_ref[j, :, pl.ds(QUARTER * a, QUARTER)] = rounded[6 * j : 6 * j + 6].astype(BF16)
    acc_ref[...] = jnp.zeros_like(acc_ref)
    source = lanes((N_LAT, DEVS), 0)
    slot = lanes((N_LAT, DEVS), 1)
    mine = jnp.where(slot // CAP == source, send_ref[...] % 2, 0).astype(F32).astype(BF16)
    spread = (lanes((DEVS, 128), 0) % CAP == lanes((DEVS, 128), 1) // KOBS).astype(F32).astype(BF16)
    seen_ref[...] = jnp.dot(mine, spread, preferred_element_type=F32) * BLKW
    across = lanes((128, 128), 0).astype(F32)
    pair_code = lanes((64, 128), 0).astype(F32)
    slot_code = (lanes((1, 128), 1) // KOBS * 8).astype(F32)

    def observe(d):
        fields = [obs_ref[pl.ds(d * 8 + f, 1), :] for f in range(8)]
        places, tiles = [], []
        for t in range(CAP):
            block = jnp.clip(send_smem[d * CAP + t], 0, 199)
            j = (block * 1639) >> 16
            places.append(((block - 40 * j) >> 1, 6 * j))
            tiles.append(grid_ref[places[t][0], pl.ds(places[t][1], 8), :])
        blocks = jnp.concatenate(tiles, axis=0)
        offset = across - (fields[5] + seen_ref[pl.ds(d, 1), :])
        table = jnp.where(offset == 3.0, fields[3], 0.0)
        for w in (2, 1, 0):
            table = jnp.where(offset == float(w), fields[w], table)
        hot = jnp.where(pair_code == fields[4] + slot_code, 1.0, 0.0).astype(BF16)
        picks = jnp.dot(blocks.T.astype(BF16), hot, preferred_element_type=F32)
        seen = jnp.sum(picks * table, axis=0, keepdims=True)
        weighted = (seen - fields[6]) * fields[7]
        seen_ref[pl.ds(d, 1), :] = weighted
        back = table * weighted
        high = back.astype(BF16)
        rest = (back - high.astype(F32)).astype(BF16)
        spreads = lax.dot_general(hot, high, NT, preferred_element_type=F32) + lax.dot_general(
            hot, rest, NT, preferred_element_type=F32
        )
        for t in range(CAP):
            chunk, row = places[t]
            acc_ref[chunk, pl.ds(row, 8), :] += spreads[8 * t : 8 * t + 8]

    def observe_group(k, carry):
        for d in range(4):
            observe(k * 4 + d)
        return carry

    lax.fori_loop(0, N_LAT // 4, observe_group, 0)
    grads = [
        jnp.concatenate([acc_ref[a * 5 + u] for u in range(5)], axis=1).astype(BF16).astype(F32) for a in range(4)
    ]
    even, other = grads[0] + grads[2], grads[1] + grads[3]
    folded = jnp.concatenate([even + other, even - other, grads[0] - grads[2], grads[1] - grads[3]], axis=0)
    back = lax.dot_general(folded.astype(BF16), phase_ref[...], NT, preferred_element_type=F32)
    for i in range(ORDERS):
        zero, two, odd, turned = masks[i]
        by_cos = back[:, i * DEVS : (i + 1) * DEVS]
        by_sin = back[:, (ORDERS + i) * DEVS : (ORDERS + i + 1) * DEVS]
        grouped_ref[2 * i] = by_cos[:32] * zero + by_cos[32:64] * two + by_cos[64:96] * odd + by_sin[96:] * turned
        grouped_ref[2 * i + 1] = by_sin[:32] * zero + by_sin[32:64] * two + by_sin[64:96] * odd - by_cos[96:] * turned
    for g in range(2 * ORDERS):
        for j in range(ROWS):
            turned_ref[pl.ds(64 * j + 6 * g, 6), :] = grouped_ref[g, pl.ds(6 * j, 6), :]
    for jj in range(3):
        wide_ref[pl.ds(jj, DEVS, stride=4), :] = turned_ref[pl.ds(128 * jj, 128), :].T
    for o in range(DEVS // N_LAT):
        wide_ref[pl.ds(4 * N_LAT * o + 3, N_LAT, stride=4), :] = seen_ref[...]
    out_ref[...] = wide_ref[...].astype(BF16)


def analysis_kernel(
    rows_ref, lookup_ref, control_ref, legendre_ref, weighted_ref, grad_ref, table_ref, wide_ref, turned_ref, half_ref, spectral_ref, sems
):
    copies = start_tables(legendre_ref, table_ref, sems)
    wide_ref[...] = rows_ref[...].astype(F32)
    first = lax.axis_index("order") * (4 * N_LAT)
    weighted_ref[...] = wide_ref[pl.ds(first + 3, N_LAT, stride=4), :]
    for jj in range(3):
        turned_ref[pl.ds(128 * jj, 128), :] = wide_ref[pl.ds(jj, DEVS, stride=4), :].T
    for half in range(2):
        total = jnp.zeros((64, NHALF), F32)
        for j in range(ROWS):
            piece = turned_ref[pl.ds(64 * j, 64), pl.ds(128 * half, 128)].astype(BF16)
            total = total + jnp.dot(piece, row_picks(half, j), preferred_element_type=F32)
        half_ref[half] = total
    signs = alternate_signs()
    for i in range(ORDERS):
        both = jnp.concatenate(
            [half_ref[0, pl.ds(12 * i, 12), :], half_ref[1, pl.ds(12 * i, 12), :]], axis=0
        ).astype(BF16)
        copies[i].wait()
        sums = lax.dot_general(both, table_ref[i], NT, preferred_element_type=F32)
        sums = sums[:12] + signs * sums[12:]
        for u in range(MM // 128):
            spectral_ref[u, pl.ds(i, 12, stride=8), :] = sums[:, 128 * u : 128 * u + 128]
    for c in range(2):
        for f in range(3):
            for b in range(2):
                for u in range(MM // 128):
                    at = pl.ds(128 * u, 128)
                    total = control_ref[c * 6 + f * 2 + b, :, at]
                    for a in range(2):
                        factor = lookup_ref[u, pl.ds((f * 4 + a * 2 + b) * 8, ORDERS), :]
                        total = total + factor * spectral_ref[u, pl.ds((c * 6 + f * 2 + a) * 8, ORDERS), :]
                    grad_ref[c * 6 + f * 2 + b, :, at] = total


VMEM = pl.BlockSpec(memory_space=pltpu.VMEM)
SMEM = pl.BlockSpec(memory_space=pltpu.SMEM)
HBM = pl.BlockSpec(memory_space=pl.ANY)


def grant(mib):
    return pltpu.CompilerParams(vmem_limit_bytes=mib * 1024 * 1024)


def shards(
    control, vertical, legendre, order_assign, send_list, used_slot_counts, obs_count, obs_var, obs_col, obs_weight, obs_value, obs_error
):
    shape = jax.ShapeDtypeStruct
    with jax.named_scope("pack_obs"):
        packed = pl.pallas_call(
            pack_obs, out_shape=shape((DEVS, 128), F32), in_specs=[VMEM] * 7, out_specs=VMEM, name="pack_obs",
        )(
            obs_var.reshape(N_LAT, 128), obs_col.reshape(N_LAT, 128), obs_weight.reshape(4, N_LAT, 128),
            obs_value.reshape(N_LAT, 128), obs_error.reshape(N_LAT, 128),
            used_slot_counts.reshape(1, N_LAT), obs_count.reshape(1, DEVS),
        )
    obs = lax.all_to_all(packed.reshape(N_LAT, 8, 128), "lat", split_axis=0, concat_axis=0, tiled=True)
    coeffs = control.reshape(12, ORDERS, MM)
    with jax.named_scope("synthesis"):
        outgoing, lookup = pl.pallas_call(
            synth_kernel,
            out_shape=(shape((4 * DEVS, 128), BF16), shape((MM // 128, 96, 128), F32)),
            in_specs=[SMEM, VMEM, VMEM, HBM],
            out_specs=(VMEM, VMEM),
            scratch_shapes=[
                pltpu.VMEM((ORDERS, MM, NHALF), BF16),
                pltpu.VMEM((16, 2 * MM + 128), F32),
                pltpu.VMEM((MM // 128, 96, 128), F32),
                pltpu.VMEM((2, 64, NHALF), F32),
                pltpu.VMEM((4 * DEVS, 128), F32),
                pltpu.SemaphoreType.DMA((ORDERS,)),
            ],
            compiler_params=grant(28),
            cost_estimate=pl.CostEstimate(flops=2 * 24 * 5 * MM * NHALF, bytes_accessed=9 << 20, transcendentals=0),
            name="synthesis",
        )(order_assign, vertical, coeffs, legendre)
    arrived = lax.all_to_all(
        outgoing.reshape(DEVS, 4, 128), ("order", "lat"), split_axis=0, concat_axis=0, tiled=True
    ).reshape(4 * DEVS, 128)
    by_device = order_assign.reshape(DEVS, ORDERS)
    with jax.named_scope("phases"):
        phases = pl.pallas_call(
            phase_kernel,
            out_shape=shape((2 * ORDERS * DEVS, QUARTER), BF16),
            in_specs=[VMEM],
            out_specs=VMEM,
            compiler_params=grant(16),
            cost_estimate=pl.CostEstimate(flops=40_000_000, bytes_accessed=4 << 20, transcendentals=0),
            name="phases",
        )(by_device)
    with jax.named_scope("middle"):
        increment, returning = pl.pallas_call(
            middle_kernel,
            out_shape=(shape((ROWS, VARS, NLON), BF16), shape((4 * DEVS, 128), BF16)),
            in_specs=[SMEM, VMEM, VMEM, VMEM, VMEM, VMEM],
            out_specs=(VMEM, VMEM),
            scratch_shapes=[
                pltpu.VMEM((4 * DEVS, 128), F32),
                pltpu.VMEM((384, DEVS), F32),
                pltpu.VMEM((2 * ORDERS, 32, DEVS), F32),
                pltpu.VMEM((128, 2 * ORDERS * DEVS), BF16),
                pltpu.VMEM((CHUNKS, 32, 128), F32),
                pltpu.VMEM((CHUNKS, 32, 128), F32),
                pltpu.VMEM((N_LAT, 128), F32),
            ],
            compiler_params=grant(28),
            name="middle",
        )(send_list.reshape(DEVS), send_list.reshape(1, DEVS), by_device.T, obs.reshape(DEVS, 128), arrived, phases)
    returned = lax.all_to_all(
        returning.reshape(DEVS, 4, 128), ("order", "lat"), split_axis=0, concat_axis=0, tiled=True
    ).reshape(4 * DEVS, 128)
    with jax.named_scope("analysis"):
        weighted, gradient = pl.pallas_call(
            analysis_kernel,
            out_shape=(shape((N_LAT, 128), F32), shape((12, ORDERS, MM), F32)),
            in_specs=[VMEM, VMEM, VMEM, HBM],
            out_specs=(VMEM, VMEM),
            scratch_shapes=[
                pltpu.VMEM((ORDERS, MM, NHALF), BF16),
                pltpu.VMEM((4 * DEVS, 128), F32),
                pltpu.VMEM((384, DEVS), F32),
                pltpu.VMEM((2, 64, NHALF), F32),
                pltpu.VMEM((MM // 128, 96, 128), F32),
                pltpu.SemaphoreType.DMA((ORDERS,)),
            ],
            compiler_params=grant(28),
            name="analysis",
        )(returned, lookup, coeffs, legendre)
    return increment, weighted.reshape(obs_value.shape), gradient.reshape(control.shape)


def solution(mesh):
    return jax.shard_map(
        shards,
        mesh=mesh,
        in_specs=(
            P(None, None, None, ("order", "lat"), None),
            P(),
            P(("order", "lat"), None, None),
            P(),
            P("order", "lat", None),
            P("order", "lat", None),
            P("order", "lat", None),
            P("order", "lat", None),
            P("order", "lat", None),
            P(None, "order", "lat", None),
            P("order", "lat", None),
            P("order", "lat", None),
        ),
        out_specs=(
            P(("order", "lat"), None, None),
            P("order", "lat", None),
            P(None, None, None, ("order", "lat"), None),
        ),
        check_vma=False,
    )
```

profile of v0, /device:TPU:1, one launch (start us, length us, event | category | flops | bytes accessed | tf_op | source)
XLA Modules:
  0.0 101.6 jit_solution(16988371083509399328)
XLA Ops:
  0.6 0.0 copy-start.8
  0.6 0.0 copy-start.9
  0.7 1.7 %pack_obs.1 = f32[256,128]{1,0:T(8,128)} custom-call(s32[32,128]{1,0:T(8,128)} %bitcast.30, s32[32,128]{1,0:T(8,128)} %bitcast.31, f32[4,32,128]{2,1,0:T(8,128)} %bitcast.29, f32[32,128]{1,0:T(8,128)} %bitcast.32, f32[32,128]{1,0:T(8,128)} %bitcast.33, s32[1,32]{1,0:T(1,128)} %bitcast.35, s32[1,256]{1,0:T(1,128)} %bitcast.34), custom_call_target="tpu_custom_call" | custom-call | tf_op jit(solution)/shard_map/pack_obs/pack_obs/pallas_call | solution.py:307
  2.4 14.5 %all-to-all-start = ((f32[32,8,128]{2,1,0:T(8,128)}), f32[32,8,128]{2,1,0:T(8,128)S(1)}, u32[]{:S(2)}, u32[]{:S(2)}) async-start(f32[32,8,128]{2,1,0:T(8,128)} %bitcast.28), calls=%async_computation | async-start | bytes 262144 | tf_op jit(solution)/shard_map/all_to_all | solution.py:314
  16.9 1.0 %copy.19 = f32[2,3,2,5,1280]{4,3,2,1,0:T(8,128)S(1)} copy(f32[2,3,2,5,1280]{4,2,3,1,0:T(2,128)} %param.12) | data formatting | bytes 614400 | tf_op args[0]
  17.9 0.0 copy-start
  17.9 3.3 %copy-done = bf16[5,1280,640]{2,1,0:T(8,128)(2,1)S(1)} copy-done((bf16[5,1280,640]{2,1,0:T(8,128)(2,1)S(1)}, bf16[5,1280,640]{2,1,0:T(8,128)(2,1)}, u32[]{:S(2)}) %copy-start) | copy-done | bytes 8192024
  21.2 0.0 copy-start.6
  21.2 0.8 copy-done.6
  22.1 0.0 copy-start.7
  22.1 0.7 copy-done.7
  22.8 5.5 %synthesis.1 = (bf16[1024,128]{1,0:T(8,128)(2,1)}, f32[10,96,128]{2,1,0:T(8,128)S(1)}) custom-call(s32[1280]{0:T(1024)S(1)} %copy-done.7, f32[3,2,2,1280]{3,2,1,0:T(2,128)S(1)} %copy-done.6, f32[12,5,1280]{2,1,0:T(8,128)S(1)} %bitcast.19, bf16[5,1280,640]{2,1,0:T(8,128)(2,1)S(1)} %copy-done), custom_call_target="tpu_custom_call" | custom-call | flops 196608000 | bytes 9437184 | tf_op jit(solution)/shard_map/synthesis/synthesis/pallas_call | solution.py:317
  28.3 0.0 copy-start.2
  28.3 0.8 copy-done.2
  29.1 0.0 copy-start.4
  29.1 0.8 copy-done.4
  29.9 0.0 all-to-all-done
  29.9 14.4 %all-to-all-start.1 = ((bf16[256,4,128]{2,1,0:T(4,128)(2,1)}), bf16[256,4,128]{2,1,0:T(4,128)(2,1)}, u32[]{:S(2)}, u32[]{:S(2)}) async-start(bf16[256,4,128]{2,1,0:T(4,128)(2,1)} %bitcast.13), calls=%async_computation.1 | async-start | bytes 524288 | tf_op jit(solution)/shard_map/all_to_all | solution.py:334
  44.2 0.0 copy-done.8
  44.2 0.2 reshape.65.order_ref
  44.4 0.1 copy.18
  44.5 6.9 %phases.1.phase_ref = bf16[2560,640]{1,0:T(8,128)(2,1)S(1)} custom-call(s32[256,5]{1,0:T(8,128)S(1)} %reshape.65.order_ref), custom_call_target="tpu_custom_call" | custom-call | flops 40000000 | bytes 4194304 | tf_op jit(solution)/shard_map/phases/phases/pallas_call | solution.py:339
  51.4 7.6 %all-to-all-done.1 = bf16[256,4,128]{2,1,0:T(4,128)(2,1)} async-done(((bf16[256,4,128]{2,1,0:T(4,128)(2,1)}), bf16[256,4,128]{2,1,0:T(4,128)(2,1)}, u32[]{:S(2)}, u32[]{:S(2)}) %all-to-all-start.1) | async-done | bytes 262176 | tf_op jit(solution)/shard_map/all_to_all | solution.py:334
  59.0 0.0 copy-done.9
  59.0 9.6 %middle.1 = (bf16[5,6,2560]{2,1,0:T(8,128)(2,1)}, bf16[1024,128]{1,0:T(8,128)(2,1)S(1)}) custom-call(s32[256]{0:T(256)S(1)} %bitcast.26, s32[1,256]{1,0:T(1,128)S(1)} %bitcast.27, s32[5,256]{1,0:T(8,128)S(1)} %bitcast.25, f32[256,128]{1,0:T(8,128)S(1)} %bitcast.22, bf16[1024,128]{1,0:T(8,128)(2,1)} %bitcast.14.rows_ref, bf16[2560,640]{1,0:T(8,128)(2,1)S(1)} %phases.1.phase_ref), custom_call_target="tpu_custom_call" | custom-call | tf_op jit(solution)/shard_map/middle/middle/pallas_call | solution.py:349
  68.6 21.6 %all_to_all.15 = bf16[256,4,128]{2,1,0:T(4,128)(2,1)S(1)} all-to-all(bf16[256,4,128]{2,1,0:T(4,128)(2,1)S(1)} %bitcast.24), channel_id=1, replica_groups=mesh['order'=8,'lat'=32] {'order','lat'}, dimensions={0} | all-to-all | bytes 524288 | tf_op jit(solution)/shard_map/all_to_all | solution.py:366
  90.3 0.0 copy-start.1
  90.3 3.3 %copy-done.1 = bf16[5,1280,640]{2,1,0:T(8,128)(2,1)S(1)} copy-done((bf16[5,1280,640]{2,1,0:T(8,128)(2,1)S(1)}, bf16[5,1280,640]{2,1,0:T(8,128)(2,1)}, u32[]{:S(2)}) %copy-start.1) | copy-done | bytes 8192024
  93.6 0.0 copy-start.3
  93.6 1.0 %copy-done.3 = f32[2,3,2,5,1280]{4,3,2,1,0:T(8,128)S(1)} copy-done((f32[2,3,2,5,1280]{4,3,2,1,0:T(8,128)S(1)}, f32[2,3,2,5,1280]{4,3,2,1,0:T(8,128)}, u32[]{:S(2)}) %copy-start.3) | copy-done | bytes 307224
  94.6 0.0 copy-start.5
  94.6 1.0 %copy-done.5 = f32[10,96,128]{2,1,0:T(8,128)S(1)} copy-done((f32[10,96,128]{2,1,0:T(8,128)S(1)}, f32[10,96,128]{2,1,0:T(8,128)}, u32[]{:S(2)}) %copy-start.5) | copy-done | bytes 491544
  95.7 5.0 %analysis.1 = (f32[32,128]{1,0:T(8,128)}, f32[12,5,1280]{2,1,0:T(8,128)S(1)}) custom-call(bf16[1024,128]{1,0:T(8,128)(2,1)S(1)} %bitcast.21, f32[10,96,128]{2,1,0:T(8,128)S(1)} %copy-done.5, f32[12,5,1280]{2,1,0:T(8,128)S(1)} %bitcast.20, bf16[5,1280,640]{2,1,0:T(8,128)(2,1)S(1)} %copy-done.1), custom_call_target="tpu_custom_call" | custom-call | tf_op jit(solution)/shard_map/analysis/analysis/pallas_call | solution.py:370
  100.7 0.9 copy.20
Async XLA Ops:
  0.6 43.6 %copy-start.8 = (s32[1280]{0:T(1024)S(1)}, s32[1280]{0:T(1024)}, u32[]{:S(2)}) copy-start(s32[1280]{0:T(1024)} %order_ref.1) | copy-start | bytes 15364
  0.6 58.4 %copy-start.9 = (s32[1,1,256]{2,1,0:T(1,128)S(1)}, s32[1,1,256]{2,1,0:T(1,128)}, u32[]{:S(2)}) copy-start(s32[1,1,256]{2,1,0:T(1,128)} %param.16) | copy-start | bytes 3076
  2.4 27.5 %all-to-all-start = ((f32[32,8,128]{2,1,0:T(8,128)}), f32[32,8,128]{2,1,0:T(8,128)S(1)}, u32[]{:S(2)}, u32[]{:S(2)}) async-start(f32[32,8,128]{2,1,0:T(8,128)} %bitcast.28), calls=%async_computation | async-start | bytes 262144 | tf_op jit(solution)/shard_map/all_to_all | solution.py:314
  17.9 3.3 %copy-start = (bf16[5,1280,640]{2,1,0:T(8,128)(2,1)S(1)}, bf16[5,1280,640]{2,1,0:T(8,128)(2,1)}, u32[]{:S(2)}) copy-start(bf16[5,1280,640]{2,1,0:T(8,128)(2,1)} %legendre_ref.3) | copy-start | bytes 24576004
  21.2 0.8 copy-start.6
  22.1 0.7 copy-start.7
  28.3 0.8 copy-start.2
  29.1 0.8 copy-start.4
  29.9 29.1 %all-to-all-start.1 = ((bf16[256,4,128]{2,1,0:T(4,128)(2,1)}), bf16[256,4,128]{2,1,0:T(4,128)(2,1)}, u32[]{:S(2)}, u32[]{:S(2)}) async-start(bf16[256,4,128]{2,1,0:T(4,128)(2,1)} %bitcast.13), calls=%async_computation.1 | async-start | bytes 524288 | tf_op jit(solution)/shard_map/all_to_all | solution.py:334
  90.3 3.3 %copy-start.1 = (bf16[5,1280,640]{2,1,0:T(8,128)(2,1)S(1)}, bf16[5,1280,640]{2,1,0:T(8,128)(2,1)}, u32[]{:S(2)}) copy-start(bf16[5,1280,640]{2,1,0:T(8,128)(2,1)} %legendre_ref.3) | copy-start | bytes 24576004
  93.6 1.0 %copy-start.3 = (f32[2,3,2,5,1280]{4,3,2,1,0:T(8,128)S(1)}, f32[2,3,2,5,1280]{4,3,2,1,0:T(8,128)}, u32[]{:S(2)}) copy-start(f32[2,3,2,5,1280]{4,3,2,1,0:T(8,128)} %copy-done.2) | copy-start | bytes 921604
  94.6 1.0 %copy-start.5 = (f32[10,96,128]{2,1,0:T(8,128)S(1)}, f32[10,96,128]{2,1,0:T(8,128)}, u32[]{:S(2)}) copy-start(f32[10,96,128]{2,1,0:T(8,128)} %copy-done.4) | copy-start | bytes 1474564
where the time goes:
time: 102 us
  starting transfers between devices  28.9 us (28%)
  Pallas kernels  28.8 us (28%)
  blocking collectives  21.6 us (21%)
  local copies, waits for them, and re-layouts  14 us (14%)
  waiting for transfers between devices  7.56 us (7%)
    all_to_all x1, blocking collectives, shards(): lax.all_to_all(returning.reshape(DEVS, 4, 128), ('order', 'lat'), split_a...  21.6 us
    all_to_all x1, starting transfers between devices, shards(): lax.all_to_all(packed.reshape(N_LAT, 8, 128), 'lat', split_axis=0, concat...  14.5 us
    all_to_all x1, starting transfers between devices, shards(): lax.all_to_all(outgoing.reshape(DEVS, 4, 128), ('order', 'lat'), split_ax...  14.4 us
    unnamed x22, local copies, waits for them, and re-layouts  13.7 us
    pallas_call x1, Pallas kernels, shards(): pl.pallas_call(middle_kernel, out_shape=(shape((ROWS, VARS, NLON), BF16),...  9.63 us
    all_to_all x1, waiting for transfers between devices, shards(): lax.all_to_all(outgoing.reshape(DEVS, 4, 128), ('order', 'lat'), split_ax...  7.56 us
    pallas_call x1, Pallas kernels, shards(): pl.pallas_call(phase_kernel, out_shape=shape((2 * ORDERS * DEVS, QUARTER)...  6.9 us
    pallas_call x1, Pallas kernels, shards(): pl.pallas_call(synth_kernel, out_shape=(shape((4 * DEVS, 128), BF16), sha...  5.51 us
  transfers between devices with their start and end apart: 2, of which 1 were waited for; matrix products, arithmetic and copies ran while one was open for 1% of the time, Pallas kernels for 12%

commit v1 on v0

--- a/solution.py
+++ b/solution.py
@@ -19,6 +19,7 @@
 ROWS = 5
 ORDERS = 5
 DEVS = 256
+GROUP = 32
 N_LAT = 32
 CHUNKS = NLON // 128
 F32 = jnp.float32
@@ -30,7 +31,10 @@
     return lax.broadcasted_iota(jnp.int32, shape, axis)
 
 
-def pack_obs(var_ref, col_ref, weight_ref, value_ref, error_ref, used_ref, count_ref, out_ref):
+def pack_obs(var_ref, col_ref, weight_ref, value_ref, error_ref, used_ref, count_ref, send_ref, out_ref, place_ref):
+    block = jnp.clip(send_ref[...], 0, 199)
+    row = (block * 1639) >> 16
+    place_ref[...] = (block - 40 * row) * 32 + row * 6
     source = lanes((N_LAT, DEVS), 0)
     slot = lanes((N_LAT, DEVS), 1)
     mine = jnp.where(slot // CAP == source, count_ref[...].astype(F32), 0.0).astype(BF16)
@@ -56,51 +60,70 @@
     return jnp.where(at == want, 1.0, 0.0).astype(BF16)
 
 
+def alternate_signs():
+    return jnp.where(lanes((1, MM), 1) % 2 == 0, 1.0, -1.0)
+
+
 def start_tables(legendre_ref, table_ref, sems):
+    copies = [pltpu.make_async_copy(legendre_ref.at[i], table_ref.at[i], sems.at[i]) for i in range(ORDERS)]
+    for copy in copies:
+        copy.start(priority=1)
+    return copies
+
+
+def start_small(order_ref, vertical_ref, control_ref, order_smem, vertical_buf, control_buf, sems):
     copies = [
-        pltpu.make_async_copy(legendre_ref.at[i], table_ref.at[i], sems.at[i]) for i in range(ORDERS)
+        pltpu.make_async_copy(order_ref, order_smem, sems.at[0]),
+        pltpu.make_async_copy(vertical_ref, vertical_buf, sems.at[1]),
+        pltpu.make_async_copy(control_ref, control_buf, sems.at[2]),
     ]
     for copy in copies:
         copy.start()
     return copies
 
 
-def alternate_signs():
-    return jnp.where(lanes((1, MM), 1) % 2 == 0, 1.0, -1.0)
-
-
-def synth_kernel(
-    order_ref, vertical_ref, control_ref, legendre_ref, out_ref, lookup_ref, table_ref, padded_ref, mixed_ref, half_ref, rows_ref, sems
-):
-    copies = start_tables(legendre_ref, table_ref, sems)
-    first = (lax.axis_index("order") * N_LAT + lax.axis_index("lat")) * ORDERS
+def pad_vertical(vertical_buf, padded_ref):
     padded_ref[...] = jnp.zeros_like(padded_ref)
     for f in range(3):
         for a in range(2):
-            padded_ref[pl.ds(f * 4 + a * 2, 2), pl.ds(0, MM)] = vertical_ref[f, a]
-    for i in range(ORDERS):
-        order = order_ref[first + i]
-        base = pl.multiple_of((order // 128) * 128, 128)
-        window = padded_ref[:, pl.ds(base, MM + 128)]
-        window = pltpu.roll(window, (MM + 128) - order % 128, 1)
-        for u in range(MM // 128):
-            lookup_ref[u, pl.ds(i, 12, stride=8), :] = window[:12, 128 * u : 128 * u + 128]
-    for c in range(2):
-        for f in range(3):
-            for a in range(2):
-                for u in range(MM // 128):
-                    at = pl.ds(128 * u, 128)
-                    mix = lookup_ref[u, pl.ds((f * 4 + a * 2) * 8, ORDERS), :] * control_ref[c * 6 + f * 2, :, at]
-                    other = lookup_ref[u, pl.ds((f * 4 + a * 2 + 1) * 8, ORDERS), :]
-                    mix = mix + other * control_ref[c * 6 + f * 2 + 1, :, at]
-                    mixed_ref[u, pl.ds((c * 6 + f * 2 + a) * 8, ORDERS), :] = mix
+            padded_ref[pl.ds(f * 4 + a * 2, 2), pl.ds(0, MM)] = vertical_buf[f, a]
+
+
+def lookup_rows(order, padded_ref):
+    base = pl.multiple_of((order // 128) * 128, 128)
+    window = padded_ref[:, pl.ds(base, MM + 128)]
+    return pltpu.roll(window, (MM + 128) - order % 128, 1)[:, :MM]
+
+
+def first_slot():
+    return (lax.axis_index("order") * N_LAT + lax.axis_index("lat")) * ORDERS
+
+
+def synth_kernel(
+    order_ref, vertical_ref, control_ref, legendre_ref, out_ref,
+    order_smem, vertical_buf, control_buf, table_ref, padded_ref, mixed_ref, half_ref, rows_ref, small_sems, sems,
+):
+    small = start_small(order_ref, vertical_ref, control_ref, order_smem, vertical_buf, control_buf, small_sems)
+    copies = start_tables(legendre_ref, table_ref, sems)
+    half_ref[...] = jnp.zeros_like(half_ref)
+    for copy in small:
+        copy.wait()
+    pad_vertical(vertical_buf, padded_ref)
     signs = alternate_signs()
-    half_ref[...] = jnp.zeros_like(half_ref)
-    for i in range(ORDERS):
-        coeffs = jnp.concatenate([mixed_ref[u, pl.ds(i, 12, stride=8), :] for u in range(MM // 128)], axis=1)
-        signed = jnp.concatenate([coeffs, coeffs * signs], axis=0).astype(BF16)
+    for i in range(ORDERS):
+        lookup = lookup_rows(order_smem[first_slot() + i], padded_ref)
+        rows = []
+        for c in range(2):
+            for f in range(3):
+                coeffs = control_buf[c, f, i]
+                for a in range(2):
+                    at = f * 4 + a * 2
+                    rows.append(jnp.sum(lookup[at : at + 2] * coeffs, axis=0, keepdims=True))
+        coeffs = jnp.concatenate(rows, axis=0)
+        mixed_ref[i] = jnp.concatenate([coeffs, coeffs * signs], axis=0).astype(BF16)
+    for i in range(ORDERS):
         copies[i].wait()
-        both = jnp.dot(signed, table_ref[i], preferred_element_type=F32)
+        both = jnp.dot(mixed_ref[i], table_ref[i], preferred_element_type=F32)
         half_ref[0, pl.ds(12 * i, 12), :] = both[:12]
         half_ref[1, pl.ds(12 * i, 12), :] = both[12:]
     low = lanes((128, 128), 1) < 64
@@ -159,8 +182,8 @@
 
 
 def middle_kernel(
-    send_smem, send_ref, order_ref, obs_ref, rows_ref, phase_ref, inc_ref, out_ref,
-    wide_ref, turned_ref, grouped_ref, lhs_ref, grid_ref, acc_ref, seen_ref,
+    place_smem, order_ref, obs_ref, rows_ref, phase_ref, inc_ref, out_ref,
+    wide_ref, turned_ref, grouped_ref, lhs_ref, grid_ref, acc_ref, seen_ref, table_ref, hot_ref,
 ):
     wide_ref[...] = rows_ref[...].astype(F32)
     for jj in range(3):
@@ -184,55 +207,56 @@
     for a in range(4):
         rounded = quarters[a].astype(BF16).astype(F32)
         for u in range(5):
-            grid_ref[a * 5 + u] = rounded[:, 128 * u : 128 * u + 128]
+            pair = rounded[:, 128 * u : 128 * u + 128]
+            grid_ref[pl.ds((a * 5 + u) * 64, 32), :] = pair
+            grid_ref[pl.ds((a * 5 + u) * 64 + 32, 32), :] = pltpu.roll(pair, BLKW, 1)
         for j in range(ROWS):
             inc_ref[j, :, pl.ds(QUARTER * a, QUARTER)] = rounded[6 * j : 6 * j + 6].astype(BF16)
     acc_ref[...] = jnp.zeros_like(acc_ref)
-    source = lanes((N_LAT, DEVS), 0)
-    slot = lanes((N_LAT, DEVS), 1)
-    mine = jnp.where(slot // CAP == source, send_ref[...] % 2, 0).astype(F32).astype(BF16)
-    spread = (lanes((DEVS, 128), 0) % CAP == lanes((DEVS, 128), 1) // KOBS).astype(F32).astype(BF16)
-    seen_ref[...] = jnp.dot(mine, spread, preferred_element_type=F32) * BLKW
-    across = lanes((128, 128), 0).astype(F32)
+    across = lanes((BLKW, 128), 0).astype(F32)
     pair_code = lanes((64, 128), 0).astype(F32)
     slot_code = (lanes((1, 128), 1) // KOBS * 8).astype(F32)
 
-    def observe(d):
-        fields = [obs_ref[pl.ds(d * 8 + f, 1), :] for f in range(8)]
-        places, tiles = [], []
-        for t in range(CAP):
-            block = jnp.clip(send_smem[d * CAP + t], 0, 199)
-            j = (block * 1639) >> 16
-            places.append(((block - 40 * j) >> 1, 6 * j))
-            tiles.append(grid_ref[places[t][0], pl.ds(places[t][1], 8), :])
-        blocks = jnp.concatenate(tiles, axis=0)
-        offset = across - (fields[5] + seen_ref[pl.ds(d, 1), :])
+    def look(d):
+        fields = [obs_ref[pl.ds(d * 8 + f, 1), :] for f in range(6)]
+        tiles = [grid_ref[pl.ds(place_smem[d * CAP + t], 8), :] for t in range(CAP)]
+        offset = across - fields[5]
         table = jnp.where(offset == 3.0, fields[3], 0.0)
         for w in (2, 1, 0):
             table = jnp.where(offset == float(w), fields[w], table)
         hot = jnp.where(pair_code == fields[4] + slot_code, 1.0, 0.0).astype(BF16)
-        picks = jnp.dot(blocks.T.astype(BF16), hot, preferred_element_type=F32)
-        seen = jnp.sum(picks * table, axis=0, keepdims=True)
-        weighted = (seen - fields[6]) * fields[7]
-        seen_ref[pl.ds(d, 1), :] = weighted
-        back = table * weighted
-        high = back.astype(BF16)
-        rest = (back - high.astype(F32)).astype(BF16)
-        spreads = lax.dot_general(hot, high, NT, preferred_element_type=F32) + lax.dot_general(
-            hot, rest, NT, preferred_element_type=F32
-        )
+        blocks = jnp.concatenate(tiles, axis=0).T[:BLKW].astype(BF16)
+        picks = jnp.dot(blocks, hot, preferred_element_type=F32)
+        table_ref[d] = table
+        hot_ref[d] = hot
+        seen_ref[pl.ds(d, 1), :] = jnp.sum(picks * table, axis=0, keepdims=True)
+
+    def add_back(d):
+        back = (table_ref[d] * seen_ref[pl.ds(d, 1), :]).astype(BF16)
+        spreads = lax.dot_general(hot_ref[d], back, NT, preferred_element_type=F32)
         for t in range(CAP):
-            chunk, row = places[t]
-            acc_ref[chunk, pl.ds(row, 8), :] += spreads[8 * t : 8 * t + 8]
-
-    def observe_group(k, carry):
-        for d in range(4):
-            observe(k * 4 + d)
-        return carry
-
-    lax.fori_loop(0, N_LAT // 4, observe_group, 0)
+            acc_ref[pl.ds(place_smem[d * CAP + t], 8), pl.ds(0, BLKW)] += spreads[8 * t : 8 * t + 8]
+
+    def in_groups(step):
+        def group(k, carry):
+            for d in range(GROUP):
+                step(k * GROUP + d)
+            return carry
+
+        lax.fori_loop(0, N_LAT // GROUP, group, 0)
+
+    in_groups(look)
+    values = obs_ref[pl.ds(6, N_LAT, stride=8), :]
+    scales = obs_ref[pl.ds(7, N_LAT, stride=8), :]
+    seen_ref[...] = (seen_ref[...] - values) * scales
+    in_groups(add_back)
+    low = lanes((32, 128), 1) < BLKW
+
+    def pair_of(u):
+        return jnp.where(low, acc_ref[pl.ds(u * 64, 32), :], pltpu.roll(acc_ref[pl.ds(u * 64 + 32, 32), :], BLKW, 1))
+
     grads = [
-        jnp.concatenate([acc_ref[a * 5 + u] for u in range(5)], axis=1).astype(BF16).astype(F32) for a in range(4)
+        jnp.concatenate([pair_of(a * 5 + u) for u in range(5)], axis=1).astype(BF16).astype(F32) for a in range(4)
     ]
     even, other = grads[0] + grads[2], grads[1] + grads[3]
     folded = jnp.concatenate([even + other, even - other, grads[0] - grads[2], grads[1] - grads[3]], axis=0)
@@ -254,8 +278,11 @@
 
 
 def analysis_kernel(
-    rows_ref, lookup_ref, control_ref, legendre_ref, weighted_ref, grad_ref, table_ref, wide_ref, turned_ref, half_ref, spectral_ref, sems
+    order_ref, vertical_ref, control_ref, legendre_ref, rows_ref, weighted_ref, grad_ref,
+    order_smem, vertical_buf, control_buf, table_ref, padded_ref, lookup_ref, wide_ref, turned_ref, half_ref, grad_buf,
+    small_sems, sems, out_sems,
 ):
+    small = start_small(order_ref, vertical_ref, control_ref, order_smem, vertical_buf, control_buf, small_sems)
     copies = start_tables(legendre_ref, table_ref, sems)
     wide_ref[...] = rows_ref[...].astype(F32)
     first = lax.axis_index("order") * (4 * N_LAT)
@@ -268,26 +295,31 @@
             piece = turned_ref[pl.ds(64 * j, 64), pl.ds(128 * half, 128)].astype(BF16)
             total = total + jnp.dot(piece, row_picks(half, j), preferred_element_type=F32)
         half_ref[half] = total
+    for copy in small:
+        copy.wait()
+    pad_vertical(vertical_buf, padded_ref)
+    for i in range(ORDERS):
+        lookup_ref[i] = lookup_rows(order_smem[first_slot() + i], padded_ref)
     signs = alternate_signs()
+    outs = []
     for i in range(ORDERS):
         both = jnp.concatenate(
             [half_ref[0, pl.ds(12 * i, 12), :], half_ref[1, pl.ds(12 * i, 12), :]], axis=0
         ).astype(BF16)
         copies[i].wait()
         sums = lax.dot_general(both, table_ref[i], NT, preferred_element_type=F32)
-        sums = sums[:12] + signs * sums[12:]
-        for u in range(MM // 128):
-            spectral_ref[u, pl.ds(i, 12, stride=8), :] = sums[:, 128 * u : 128 * u + 128]
-    for c in range(2):
-        for f in range(3):
-            for b in range(2):
-                for u in range(MM // 128):
-                    at = pl.ds(128 * u, 128)
-                    total = control_ref[c * 6 + f * 2 + b, :, at]
-                    for a in range(2):
-                        factor = lookup_ref[u, pl.ds((f * 4 + a * 2 + b) * 8, ORDERS), :]
-                        total = total + factor * spectral_ref[u, pl.ds((c * 6 + f * 2 + a) * 8, ORDERS), :]
-                    grad_ref[c * 6 + f * 2 + b, :, at] = total
+        spectral = sums[:12] + signs * sums[12:]
+        for c in range(2):
+            for f in range(3):
+                total = control_buf[c, f, i]
+                for a in range(2):
+                    at = c * 6 + f * 2 + a
+                    total = total + lookup_ref[i, pl.ds(f * 4 + a * 2, 2), :] * spectral[at : at + 1]
+                grad_buf[i, c, f] = total
+        outs.append(pltpu.make_async_copy(grad_buf.at[i], grad_ref.at[:, :, i], out_sems.at[i]))
+        outs[i].start()
+    for out in outs:
+        out.wait()
 
 
 VMEM = pl.BlockSpec(memory_space=pltpu.VMEM)
@@ -304,30 +336,41 @@
 ):
     shape = jax.ShapeDtypeStruct
     with jax.named_scope("pack_obs"):
-        packed = pl.pallas_call(
-            pack_obs, out_shape=shape((DEVS, 128), F32), in_specs=[VMEM] * 7, out_specs=VMEM, name="pack_obs",
+        packed, places = pl.pallas_call(
+            pack_obs,
+            out_shape=(shape((DEVS, 128), F32), shape((1, DEVS), jnp.int32)),
+            in_specs=[VMEM] * 8,
+            out_specs=(VMEM, VMEM),
+            name="pack_obs",
         )(
             obs_var.reshape(N_LAT, 128), obs_col.reshape(N_LAT, 128), obs_weight.reshape(4, N_LAT, 128),
             obs_value.reshape(N_LAT, 128), obs_error.reshape(N_LAT, 128),
-            used_slot_counts.reshape(1, N_LAT), obs_count.reshape(1, DEVS),
+            used_slot_counts.reshape(1, N_LAT), obs_count.reshape(1, DEVS), send_list.reshape(1, DEVS),
         )
     obs = lax.all_to_all(packed.reshape(N_LAT, 8, 128), "lat", split_axis=0, concat_axis=0, tiled=True)
-    coeffs = control.reshape(12, ORDERS, MM)
+    coeffs = control.transpose(0, 1, 3, 2, 4)
+    small_scratch = [
+        pltpu.SMEM((MM,), jnp.int32),
+        pltpu.VMEM(vertical.shape, F32),
+        pltpu.VMEM(coeffs.shape, F32),
+        pltpu.VMEM((ORDERS, MM, NHALF), BF16),
+        pltpu.VMEM((16, 2 * MM + 128), F32),
+    ]
     with jax.named_scope("synthesis"):
-        outgoing, lookup = pl.pallas_call(
+        outgoing = pl.pallas_call(
             synth_kernel,
-            out_shape=(shape((4 * DEVS, 128), BF16), shape((MM // 128, 96, 128), F32)),
-            in_specs=[SMEM, VMEM, VMEM, HBM],
-            out_specs=(VMEM, VMEM),
-            scratch_shapes=[
-                pltpu.VMEM((ORDERS, MM, NHALF), BF16),
-                pltpu.VMEM((16, 2 * MM + 128), F32),
-                pltpu.VMEM((MM // 128, 96, 128), F32),
+            out_shape=shape((4 * DEVS, 128), BF16),
+            in_specs=[HBM] * 4,
+            out_specs=VMEM,
+            scratch_shapes=small_scratch
+            + [
+                pltpu.VMEM((ORDERS, 24, MM), BF16),
                 pltpu.VMEM((2, 64, NHALF), F32),
                 pltpu.VMEM((4 * DEVS, 128), F32),
+                pltpu.SemaphoreType.DMA((3,)),
                 pltpu.SemaphoreType.DMA((ORDERS,)),
             ],
-            compiler_params=grant(28),
+            compiler_params=grant(60),
             cost_estimate=pl.CostEstimate(flops=2 * 24 * 5 * MM * NHALF, bytes_accessed=9 << 20, transcendentals=0),
             name="synthesis",
         )(order_assign, vertical, coeffs, legendre)
@@ -349,41 +392,46 @@
         increment, returning = pl.pallas_call(
             middle_kernel,
             out_shape=(shape((ROWS, VARS, NLON), BF16), shape((4 * DEVS, 128), BF16)),
-            in_specs=[SMEM, VMEM, VMEM, VMEM, VMEM, VMEM],
+            in_specs=[SMEM, VMEM, VMEM, VMEM, VMEM],
             out_specs=(VMEM, VMEM),
             scratch_shapes=[
                 pltpu.VMEM((4 * DEVS, 128), F32),
                 pltpu.VMEM((384, DEVS), F32),
                 pltpu.VMEM((2 * ORDERS, 32, DEVS), F32),
                 pltpu.VMEM((128, 2 * ORDERS * DEVS), BF16),
-                pltpu.VMEM((CHUNKS, 32, 128), F32),
-                pltpu.VMEM((CHUNKS, 32, 128), F32),
+                pltpu.VMEM((2 * CHUNKS * 32, 128), F32),
+                pltpu.VMEM((2 * CHUNKS * 32, 128), F32),
                 pltpu.VMEM((N_LAT, 128), F32),
+                pltpu.VMEM((N_LAT, BLKW, 128), F32),
+                pltpu.VMEM((N_LAT, 64, 128), BF16),
             ],
             compiler_params=grant(28),
             name="middle",
-        )(send_list.reshape(DEVS), send_list.reshape(1, DEVS), by_device.T, obs.reshape(DEVS, 128), arrived, phases)
+        )(places.reshape(DEVS), by_device.T, obs.reshape(DEVS, 128), arrived, phases)
     returned = lax.all_to_all(
         returning.reshape(DEVS, 4, 128), ("order", "lat"), split_axis=0, concat_axis=0, tiled=True
     ).reshape(4 * DEVS, 128)
     with jax.named_scope("analysis"):
         weighted, gradient = pl.pallas_call(
             analysis_kernel,
-            out_shape=(shape((N_LAT, 128), F32), shape((12, ORDERS, MM), F32)),
-            in_specs=[VMEM, VMEM, VMEM, HBM],
-            out_specs=(VMEM, VMEM),
-            scratch_shapes=[
-                pltpu.VMEM((ORDERS, MM, NHALF), BF16),
+            out_shape=(shape((N_LAT, 128), F32), shape(coeffs.shape, F32)),
+            in_specs=[HBM] * 4 + [VMEM],
+            out_specs=(VMEM, HBM),
+            scratch_shapes=small_scratch
+            + [
+                pltpu.VMEM((ORDERS, 16, MM), F32),
                 pltpu.VMEM((4 * DEVS, 128), F32),
                 pltpu.VMEM((384, DEVS), F32),
                 pltpu.VMEM((2, 64, NHALF), F32),
-                pltpu.VMEM((MM // 128, 96, 128), F32),
+                pltpu.VMEM((ORDERS, 2, 3, 2, MM), F32),
+                pltpu.SemaphoreType.DMA((3,)),
+                pltpu.SemaphoreType.DMA((ORDERS,)),
                 pltpu.SemaphoreType.DMA((ORDERS,)),
             ],
-            compiler_params=grant(28),
+            compiler_params=grant(60),
             name="analysis",
-        )(returned, lookup, coeffs, legendre)
-    return increment, weighted.reshape(obs_value.shape), gradient.reshape(control.shape)
+        )(order_assign, vertical, coeffs, legendre, returned)
+    return increment, weighted.reshape(obs_value.shape), gradient.transpose(0, 1, 3, 2, 4)
 
 
 def solution(mesh):

time: 102 us -> 87.4 us (0.86)
  local copies, waits for them, and re-layouts: 14 us -> 0.28 us
  waiting for transfers between devices: 7.56 us -> 13.5 us
  starting transfers between devices: 28.9 us -> 23.3 us
  Pallas kernels: 28.8 us -> 27.4 us
    unnamed x22 -> x4, local copies, waits for them, and re-layouts: 13.7 us -> 0.01 us
    all_to_all x1, waiting for transfers between devices: 0.01 us -> 5.76 us  [shards(): lax.all_to_all(packed.reshape(N_LAT, 8, 128), 'lat', split_axis=0, concat...]
    all_to_all x1, starting transfers between devices: 14.4 us -> 8.69 us  [shards(): lax.all_to_all(outgoing.reshape(DEVS, 4, 128), ('order', 'lat'), split_ax...]
    pallas_call x1, Pallas kernels: 9.63 us -> 5.69 us  [shards(): pl.pallas_call(middle_kernel, out_shape=(shape((ROWS, VARS, NLON), BF16),...]
    pallas_call x1, Pallas kernels: 5.05 us -> 7.33 us  [shards(): pl.pallas_call(analysis_kernel, out_shape=(shape((N_LAT, 128), F32), shap...]
  transfers between devices with their start and end apart: 2 -> 2, of which waited for: 1 -> 2; matrix products, arithmetic and copies ran while one was open for 1% -> 0% of each run, Pallas kernels for 12% -> 15%
where the time goes in v1:
time: 87.4 us; the launch traced here: 87 us
  Pallas kernels  27.4 us (31%)
  starting transfers between devices  23.3 us (27%)
  blocking collectives  21.8 us (25%)
  waiting for transfers between devices  13.5 us (15%)
    all_to_all x1, blocking collectives, shards(): lax.all_to_all(returning.reshape(DEVS, 4, 128), ('order', 'lat'), split_a...  21.8 us
    all_to_all x1, starting transfers between devices, shards(): lax.all_to_all(packed.reshape(N_LAT, 8, 128), 'lat', split_axis=0, concat...  14.6 us
    all_to_all x1, starting transfers between devices, shards(): lax.all_to_all(outgoing.reshape(DEVS, 4, 128), ('order', 'lat'), split_ax...  8.69 us
    all_to_all x1, waiting for transfers between devices, shards(): lax.all_to_all(outgoing.reshape(DEVS, 4, 128), ('order', 'lat'), split_ax...  7.7 us
    pallas_call x1, Pallas kernels, shards(): pl.pallas_call(analysis_kernel, out_shape=(shape((N_LAT, 128), F32), shap...  7.33 us
    pallas_call x1, Pallas kernels, shards(): pl.pallas_call(phase_kernel, out_shape=shape((2 * ORDERS * DEVS, QUARTER)...  6.9 us
    all_to_all x1, waiting for transfers between devices, shards(): lax.all_to_all(packed.reshape(N_LAT, 8, 128), 'lat', split_axis=0, concat...  5.76 us
    pallas_call x1, Pallas kernels, shards(): pl.pallas_call(synth_kernel, out_shape=shape((4 * DEVS, 128), BF16), in_s...  5.75 us
  transfers between devices with their start and end apart: 2, of which 2 were waited for; matrix products, arithmetic and copies ran while one was open for 0% of the time, Pallas kernels for 15%

profile of v1, /device:TPU:1, one launch (start us, length us, event | category | flops | bytes accessed | tf_op | source)
XLA Modules:
  0.0 87.0 jit_solution(7003650282022850377)
XLA Ops:
  0.6 0.0 copy-start.1
  0.6 1.7 %pack_obs.1 = (f32[256,128]{1,0:T(8,128)}, s32[1,256]{1,0:T(1,128)}) custom-call(s32[32,128]{1,0:T(8,128)} %bitcast.29, s32[32,128]{1,0:T(8,128)} %bitcast.30, f32[4,32,128]{2,1,0:T(8,128)} %bitcast.28, f32[32,128]{1,0:T(8,128)} %bitcast.31, f32[32,128]{1,0:T(8,128)} %bitcast.32, s32[1,32]{1,0:T(1,128)} %bitcast.35, s32[1,256]{1,0:T(1,128)} %bitcast.33, ...), custom_call_target="tpu_custom_call" | custom-call | tf_op jit(solution)/shard_map/pack_obs/pack_obs/pallas_call | solution.py:339
  2.4 0.0 copy-start
  2.4 14.6 %all-to-all-start = ((f32[32,8,128]{2,1,0:T(8,128)}), f32[32,8,128]{2,1,0:T(8,128)S(1)}, u32[]{:S(2)}, u32[]{:S(2)}) async-start(f32[32,8,128]{2,1,0:T(8,128)} %bitcast.27), calls=%async_computation | async-start | bytes 262144 | tf_op jit(solution)/shard_map/all_to_all | solution.py:350
  17.0 5.7 %synthesis.1 = bf16[1024,128]{1,0:T(8,128)(2,1)} custom-call(s32[1280]{0:T(1024)} %order_ref.3, f32[3,2,2,1280]{3,2,1,0:T(2,128)} %vertical_ref.3, f32[2,3,5,2,1280]{4,3,2,1,0:T(2,128)} %bitcast.23, bf16[5,1280,640]{2,1,0:T(8,128)(2,1)} %legendre_ref.3), custom_call_target="tpu_custom_call" | custom-call | flops 196608000 | bytes 9437184 | tf_op jit(solution)/shard_map/synthesis/synthesis/pallas_call | solution.py:360
  22.8 5.8 %all-to-all-done = f32[32,8,128]{2,1,0:T(8,128)S(1)} async-done(((f32[32,8,128]{2,1,0:T(8,128)}), f32[32,8,128]{2,1,0:T(8,128)S(1)}, u32[]{:S(2)}, u32[]{:S(2)}) %all-to-all-start) | async-done | bytes 131104 | tf_op jit(solution)/shard_map/all_to_all | solution.py:350
  28.5 8.7 %all-to-all-start.1 = ((bf16[256,4,128]{2,1,0:T(4,128)(2,1)}), bf16[256,4,128]{2,1,0:T(4,128)(2,1)}, u32[]{:S(2)}, u32[]{:S(2)}) async-start(bf16[256,4,128]{2,1,0:T(4,128)(2,1)} %bitcast.25), calls=%async_computation.1 | async-start | bytes 524288 | tf_op jit(solution)/shard_map/all_to_all | solution.py:377
  37.2 0.0 copy-done.1
  37.2 0.2 reshape.66.order_ref
  37.4 0.1 copy.16
  37.5 6.9 %phases.1.phase_ref = bf16[2560,640]{1,0:T(8,128)(2,1)S(1)} custom-call(s32[256,5]{1,0:T(8,128)S(1)} %reshape.66.order_ref), custom_call_target="tpu_custom_call" | custom-call | flops 40000000 | bytes 4194304 | tf_op jit(solution)/shard_map/phases/phases/pallas_call | solution.py:382
  44.4 7.7 %all-to-all-done.1 = bf16[256,4,128]{2,1,0:T(4,128)(2,1)} async-done(((bf16[256,4,128]{2,1,0:T(4,128)(2,1)}), bf16[256,4,128]{2,1,0:T(4,128)(2,1)}, u32[]{:S(2)}, u32[]{:S(2)}) %all-to-all-start.1) | async-done | bytes 262176 | tf_op jit(solution)/shard_map/all_to_all | solution.py:377
  52.1 0.0 copy-done
  52.1 5.7 %middle.1 = (bf16[5,6,2560]{2,1,0:T(8,128)(2,1)}, bf16[1024,128]{1,0:T(8,128)(2,1)S(1)}) custom-call(s32[256]{0:T(256)S(1)} %bitcast.22, s32[5,256]{1,0:T(8,128)S(1)} %bitcast.21, f32[256,128]{1,0:T(8,128)S(1)} %bitcast.19, bf16[1024,128]{1,0:T(8,128)(2,1)} %bitcast.14.rows_ref, bf16[2560,640]{1,0:T(8,128)(2,1)S(1)} %phases.1.phase_ref), custom_call_target="tpu_custom_call" | custom-call | tf_op jit(solution)/shard_map/middle/middle/pallas_call | solution.py:392
  57.8 21.8 %all_to_all.15 = bf16[256,4,128]{2,1,0:T(4,128)(2,1)} all-to-all(bf16[256,4,128]{2,1,0:T(4,128)(2,1)S(1)} %bitcast.20), channel_id=1, replica_groups=mesh['order'=8,'lat'=32] {'order','lat'}, dimensions={0} | all-to-all | bytes 524288 | tf_op jit(solution)/shard_map/all_to_all | solution.py:411
  79.5 7.3 %analysis.1 = (f32[32,128]{1,0:T(8,128)}, f32[2,3,5,2,1280]{4,3,2,1,0:T(2,128)}) custom-call(s32[1280]{0:T(1024)} %order_ref.3, f32[3,2,2,1280]{3,2,1,0:T(2,128)} %vertical_ref.3, f32[2,3,5,2,1280]{4,3,2,1,0:T(2,128)} %bitcast.24, bf16[5,1280,640]{2,1,0:T(8,128)(2,1)} %legendre_ref.3, bf16[1024,128]{1,0:T(8,128)(2,1)} %bitcast.26), custom_call_target="tpu_custom_call" | custom-call | tf_op jit(solution)/shard_map/analysis/analysis/pallas_call | solution.py:415
Async XLA Ops:
  0.6 36.6 %copy-start.1 = (s32[1280]{0:T(1024)S(1)}, s32[1280]{0:T(1024)}, u32[]{:S(2)}) copy-start(s32[1280]{0:T(1024)} %order_ref.3) | copy-start | bytes 15364
  2.4 49.7 %copy-start = (s32[1,256]{1,0:T(1,128)S(1)}, s32[1,256]{1,0:T(1,128)}, u32[]{:S(2)}) copy-start(s32[1,256]{1,0:T(1,128)} %get-tuple-element.9) | copy-start | bytes 3076
  2.4 26.1 %all-to-all-start = ((f32[32,8,128]{2,1,0:T(8,128)}), f32[32,8,128]{2,1,0:T(8,128)S(1)}, u32[]{:S(2)}, u32[]{:S(2)}) async-start(f32[32,8,128]{2,1,0:T(8,128)} %bitcast.27), calls=%async_computation | async-start | bytes 262144 | tf_op jit(solution)/shard_map/all_to_all | solution.py:350
  28.5 23.6 %all-to-all-start.1 = ((bf16[256,4,128]{2,1,0:T(4,128)(2,1)}), bf16[256,4,128]{2,1,0:T(4,128)(2,1)}, u32[]{:S(2)}, u32[]{:S(2)}) async-start(bf16[256,4,128]{2,1,0:T(4,128)(2,1)} %bitcast.25), calls=%async_computation.1 | async-start | bytes 524288 | tf_op jit(solution)/shard_map/all_to_all | solution.py:377

commit v2 on v1

--- a/solution.py
+++ b/solution.py
@@ -158,14 +158,20 @@
 
 
 def phase_kernel(order_ref, out_ref):
-    lane = lanes((DEVS, 128), 1).astype(F32)
-    for i in range(ORDERS):
-        order = order_ref[:, i : i + 1].astype(F32)
-        weight = jnp.where(order == 0.0, 1.0, 2.0)
-        fine_cos, fine_sin = turn(order * lane)
-        fine_cos, fine_sin = fine_cos * weight, fine_sin * weight
+    lane = lanes((DEVS, 128), 1)
+    coarse = jnp.zeros((DEVS, 128), F32)
+    orders = [order_ref[:, i : i + 1].astype(F32) for i in range(ORDERS)]
+    for i in range(ORDERS):
+        coarse = jnp.where(lane // 5 == i, orders[i], coarse)
+    weight = jnp.where(coarse == 0.0, 1.0, 2.0)
+    coarse_cos, coarse_sin = turn(coarse * (128 * (lane % 5)).astype(F32))
+    coarse_cos, coarse_sin = coarse_cos * weight, coarse_sin * weight
+    lane = lane.astype(F32)
+    for i in range(ORDERS):
+        fine_cos, fine_sin = turn(orders[i] * lane)
         for a in range(QUARTER // 128):
-            big_cos, big_sin = turn(order * (128.0 * a))
+            at = i * 5 + a
+            big_cos, big_sin = coarse_cos[:, at : at + 1], coarse_sin[:, at : at + 1]
             out_ref[pl.ds(i * DEVS, DEVS), pl.ds(128 * a, 128)] = (fine_cos * big_cos - fine_sin * big_sin).astype(BF16)
             out_ref[pl.ds((ORDERS + i) * DEVS, DEVS), pl.ds(128 * a, 128)] = (
                 -(fine_sin * big_cos + fine_cos * big_sin)
@@ -279,8 +285,7 @@
 
 def analysis_kernel(
     order_ref, vertical_ref, control_ref, legendre_ref, rows_ref, weighted_ref, grad_ref,
-    order_smem, vertical_buf, control_buf, table_ref, padded_ref, lookup_ref, wide_ref, turned_ref, half_ref, grad_buf,
-    small_sems, sems, out_sems,
+    order_smem, vertical_buf, control_buf, table_ref, padded_ref, lookup_ref, coeffs_ref, wide_ref, turned_ref, half_ref, both_ref, small_sems, sems,
 ):
     small = start_small(order_ref, vertical_ref, control_ref, order_smem, vertical_buf, control_buf, small_sems)
     copies = start_tables(legendre_ref, table_ref, sems)
@@ -295,31 +300,34 @@
             piece = turned_ref[pl.ds(64 * j, 64), pl.ds(128 * half, 128)].astype(BF16)
             total = total + jnp.dot(piece, row_picks(half, j), preferred_element_type=F32)
         half_ref[half] = total
+    at = lanes((160, 64), 0)
+    source = (at // 32) * 12 + (at % 16) // 2 * 2 + (at // 16) % 2
+    twice = jnp.where((lanes((160, 64), 1) == source) & (at % 16 < 12), 1.0, 0.0).astype(BF16)
+    for half in range(2):
+        both_ref[half] = jnp.dot(twice, half_ref[half].astype(BF16), preferred_element_type=F32)
     for copy in small:
         copy.wait()
-    pad_vertical(vertical_buf, padded_ref)
-    for i in range(ORDERS):
-        lookup_ref[i] = lookup_rows(order_smem[first_slot() + i], padded_ref)
-    signs = alternate_signs()
-    outs = []
-    for i in range(ORDERS):
-        both = jnp.concatenate(
-            [half_ref[0, pl.ds(12 * i, 12), :], half_ref[1, pl.ds(12 * i, 12), :]], axis=0
-        ).astype(BF16)
-        copies[i].wait()
-        sums = lax.dot_general(both, table_ref[i], NT, preferred_element_type=F32)
-        spectral = sums[:12] + signs * sums[12:]
+    padded_ref[...] = jnp.zeros_like(padded_ref)
+    for a in range(2):
         for c in range(2):
             for f in range(3):
-                total = control_buf[c, f, i]
-                for a in range(2):
-                    at = c * 6 + f * 2 + a
-                    total = total + lookup_ref[i, pl.ds(f * 4 + a * 2, 2), :] * spectral[at : at + 1]
-                grad_buf[i, c, f] = total
-        outs.append(pltpu.make_async_copy(grad_buf.at[i], grad_ref.at[:, :, i], out_sems.at[i]))
-        outs[i].start()
-    for out in outs:
-        out.wait()
+                padded_ref[pl.ds(16 * a + c * 6 + f * 2, 2), pl.ds(0, MM)] = vertical_buf[f, a]
+    for i in range(ORDERS):
+        lookup_ref[i] = lookup_rows(order_smem[first_slot() + i], padded_ref)
+        for c in range(2):
+            for f in range(3):
+                coeffs_ref[i, pl.ds(c * 6 + f * 2, 2), :] = control_buf[c, f, i]
+    signs = alternate_signs()
+    for i in range(ORDERS):
+        both = jnp.concatenate([both_ref[0, pl.ds(32 * i, 32), :], both_ref[1, pl.ds(32 * i, 32), :]], axis=0)
+        copies[i].wait()
+        sums = lax.dot_general(both.astype(BF16), table_ref[i], NT, preferred_element_type=F32)
+        spectral = (sums[:32] + signs * sums[32:]) * lookup_ref[i]
+        total = coeffs_ref[i] + (spectral[:16] + spectral[16:])
+        for c in range(2):
+            for f in range(3):
+                at = c * 6 + f * 2
+                grad_ref[c, f, i] = total[at : at + 2]
 
 
 VMEM = pl.BlockSpec(memory_space=pltpu.VMEM)
@@ -354,7 +362,6 @@
         pltpu.VMEM(vertical.shape, F32),
         pltpu.VMEM(coeffs.shape, F32),
         pltpu.VMEM((ORDERS, MM, NHALF), BF16),
-        pltpu.VMEM((16, 2 * MM + 128), F32),
     ]
     with jax.named_scope("synthesis"):
         outgoing = pl.pallas_call(
@@ -364,6 +371,7 @@
             out_specs=VMEM,
             scratch_shapes=small_scratch
             + [
+                pltpu.VMEM((16, 2 * MM + 128), F32),
                 pltpu.VMEM((ORDERS, 24, MM), BF16),
                 pltpu.VMEM((2, 64, NHALF), F32),
                 pltpu.VMEM((4 * DEVS, 128), F32),
@@ -416,16 +424,17 @@
             analysis_kernel,
             out_shape=(shape((N_LAT, 128), F32), shape(coeffs.shape, F32)),
             in_specs=[HBM] * 4 + [VMEM],
-            out_specs=(VMEM, HBM),
+            out_specs=(VMEM, VMEM),
             scratch_shapes=small_scratch
             + [
+                pltpu.VMEM((32, 2 * MM + 128), F32),
+                pltpu.VMEM((ORDERS, 32, MM), F32),
                 pltpu.VMEM((ORDERS, 16, MM), F32),
                 pltpu.VMEM((4 * DEVS, 128), F32),
                 pltpu.VMEM((384, DEVS), F32),
                 pltpu.VMEM((2, 64, NHALF), F32),
-                pltpu.VMEM((ORDERS, 2, 3, 2, MM), F32),
+                pltpu.VMEM((2, 160, NHALF), F32),
                 pltpu.SemaphoreType.DMA((3,)),
-                pltpu.SemaphoreType.DMA((ORDERS,)),
                 pltpu.SemaphoreType.DMA((ORDERS,)),
             ],
             compiler_params=grant(60),

time: 87.4 us -> 86.7 us (level)
  Pallas kernels: 27.4 us -> 22.5 us
  waiting for transfers between devices: 13.5 us -> 17.9 us
    all_to_all x1, waiting for transfers between devices: 7.7 us -> 12.2 us  [shards(): lax.all_to_all(outgoing.reshape(DEVS, 4, 128), ('order', 'lat'), split_ax...]
    pallas_call x1, Pallas kernels: 6.9 us -> 2.46 us  [shards(): pl.pallas_call(phase_kernel, out_shape=shape((2 * ORDERS * DEVS, QUARTER)...]
  transfers between devices with their start and end apart: 2 -> 2, of which waited for: 2 -> 2; matrix products, arithmetic and copies ran while one was open for 0% -> 0% of each run, Pallas kernels for 15% -> 10%
where the time goes in v2:
time: 86.7 us; the launch traced here: 86.3 us
  starting transfers between devices  23.3 us (27%)
  Pallas kernels  22.5 us (26%)
  blocking collectives  21.5 us (25%)
  waiting for transfers between devices  17.9 us (21%)
    all_to_all x1, blocking collectives, shards(): lax.all_to_all(returning.reshape(DEVS, 4, 128), ('order', 'lat'), split_a...  21.5 us
    all_to_all x1, starting transfers between devices, shards(): lax.all_to_all(packed.reshape(N_LAT, 8, 128), 'lat', split_axis=0, concat...  14.6 us
    all_to_all x1, waiting for transfers between devices, shards(): lax.all_to_all(outgoing.reshape(DEVS, 4, 128), ('order', 'lat'), split_ax...  12.2 us
    all_to_all x1, starting transfers between devices, shards(): lax.all_to_all(outgoing.reshape(DEVS, 4, 128), ('order', 'lat'), split_ax...  8.67 us
    pallas_call x1, Pallas kernels, shards(): pl.pallas_call(analysis_kernel, out_shape=(shape((N_LAT, 128), F32), shap...  6.84 us
    all_to_all x1, waiting for transfers between devices, shards(): lax.all_to_all(packed.reshape(N_LAT, 8, 128), 'lat', split_axis=0, concat...  5.76 us
    pallas_call x1, Pallas kernels, shards(): pl.pallas_call(synth_kernel, out_shape=shape((4 * DEVS, 128), BF16), in_s...  5.75 us
    pallas_call x1, Pallas kernels, shards(): pl.pallas_call(middle_kernel, out_shape=(shape((ROWS, VARS, NLON), BF16),...  5.69 us
  transfers between devices with their start and end apart: 2, of which 2 were waited for; matrix products, arithmetic and copies ran while one was open for 0% of the time, Pallas kernels for 10%

profile of v2, /device:TPU:1, one launch (start us, length us, event | category | flops | bytes accessed | tf_op | source)
XLA Modules:
  0.0 86.3 jit_solution(17196852923083635788)
XLA Ops:
  0.6 0.0 copy-start.1
  0.6 1.7 %pack_obs.1 = (f32[256,128]{1,0:T(8,128)}, s32[1,256]{1,0:T(1,128)}) custom-call(s32[32,128]{1,0:T(8,128)} %bitcast.29, s32[32,128]{1,0:T(8,128)} %bitcast.30, f32[4,32,128]{2,1,0:T(8,128)} %bitcast.28, f32[32,128]{1,0:T(8,128)} %bitcast.31, f32[32,128]{1,0:T(8,128)} %bitcast.32, s32[1,32]{1,0:T(1,128)} %bitcast.35, s32[1,256]{1,0:T(1,128)} %bitcast.33, ...), custom_call_target="tpu_custom_call" | custom-call | tf_op jit(solution)/shard_map/pack_obs/pack_obs/pallas_call | solution.py:347
  2.4 0.0 copy-start
  2.4 14.6 %all-to-all-start = ((f32[32,8,128]{2,1,0:T(8,128)}), f32[32,8,128]{2,1,0:T(8,128)S(1)}, u32[]{:S(2)}, u32[]{:S(2)}) async-start(f32[32,8,128]{2,1,0:T(8,128)} %bitcast.27), calls=%async_computation | async-start | bytes 262144 | tf_op jit(solution)/shard_map/all_to_all | solution.py:358
  17.0 5.7 %synthesis.1 = bf16[1024,128]{1,0:T(8,128)(2,1)} custom-call(s32[1280]{0:T(1024)} %order_ref.3, f32[3,2,2,1280]{3,2,1,0:T(2,128)} %vertical_ref.3, f32[2,3,5,2,1280]{4,3,2,1,0:T(2,128)} %bitcast.23, bf16[5,1280,640]{2,1,0:T(8,128)(2,1)} %legendre_ref.3), custom_call_target="tpu_custom_call" | custom-call | flops 196608000 | bytes 9437184 | tf_op jit(solution)/shard_map/synthesis/synthesis/pallas_call | solution.py:367
  22.8 5.8 %all-to-all-done = f32[32,8,128]{2,1,0:T(8,128)S(1)} async-done(((f32[32,8,128]{2,1,0:T(8,128)}), f32[32,8,128]{2,1,0:T(8,128)S(1)}, u32[]{:S(2)}, u32[]{:S(2)}) %all-to-all-start) | async-done | bytes 131104 | tf_op jit(solution)/shard_map/all_to_all | solution.py:358
  28.5 8.7 %all-to-all-start.1 = ((bf16[256,4,128]{2,1,0:T(4,128)(2,1)}), bf16[256,4,128]{2,1,0:T(4,128)(2,1)}, u32[]{:S(2)}, u32[]{:S(2)}) async-start(bf16[256,4,128]{2,1,0:T(4,128)(2,1)} %bitcast.25), calls=%async_computation.1 | async-start | bytes 524288 | tf_op jit(solution)/shard_map/all_to_all | solution.py:385
  37.2 0.0 copy-done.1
  37.2 0.2 reshape.66.order_ref
  37.4 0.1 copy.16
  37.5 2.5 %phases.1.phase_ref = bf16[2560,640]{1,0:T(8,128)(2,1)S(1)} custom-call(s32[256,5]{1,0:T(8,128)S(1)} %reshape.66.order_ref), custom_call_target="tpu_custom_call" | custom-call | flops 40000000 | bytes 4194304 | tf_op jit(solution)/shard_map/phases/phases/pallas_call | solution.py:390
  39.9 12.2 %all-to-all-done.1 = bf16[256,4,128]{2,1,0:T(4,128)(2,1)} async-done(((bf16[256,4,128]{2,1,0:T(4,128)(2,1)}), bf16[256,4,128]{2,1,0:T(4,128)(2,1)}, u32[]{:S(2)}, u32[]{:S(2)}) %all-to-all-start.1) | async-done | bytes 262176 | tf_op jit(solution)/shard_map/all_to_all | solution.py:385
  52.1 0.0 copy-done
  52.1 5.7 %middle.1 = (bf16[5,6,2560]{2,1,0:T(8,128)(2,1)}, bf16[1024,128]{1,0:T(8,128)(2,1)S(1)}) custom-call(s32[256]{0:T(256)S(1)} %bitcast.22, s32[5,256]{1,0:T(8,128)S(1)} %bitcast.21, f32[256,128]{1,0:T(8,128)S(1)} %bitcast.19, bf16[1024,128]{1,0:T(8,128)(2,1)} %bitcast.14.rows_ref, bf16[2560,640]{1,0:T(8,128)(2,1)S(1)} %phases.1.phase_ref), custom_call_target="tpu_custom_call" | custom-call | tf_op jit(solution)/shard_map/middle/middle/pallas_call | solution.py:400
  57.8 21.5 %all_to_all.15 = bf16[256,4,128]{2,1,0:T(4,128)(2,1)} all-to-all(bf16[256,4,128]{2,1,0:T(4,128)(2,1)S(1)} %bitcast.20), channel_id=1, replica_groups=mesh['order'=8,'lat'=32] {'order','lat'}, dimensions={0} | all-to-all | bytes 524288 | tf_op jit(solution)/shard_map/all_to_all | solution.py:419
  79.3 6.8 %analysis.1 = (f32[32,128]{1,0:T(8,128)}, f32[2,3,5,2,1280]{4,3,2,1,0:T(2,128)}) custom-call(s32[1280]{0:T(1024)} %order_ref.3, f32[3,2,2,1280]{3,2,1,0:T(2,128)} %vertical_ref.3, f32[2,3,5,2,1280]{4,3,2,1,0:T(2,128)} %bitcast.24, bf16[5,1280,640]{2,1,0:T(8,128)(2,1)} %legendre_ref.3, bf16[1024,128]{1,0:T(8,128)(2,1)} %bitcast.26), custom_call_target="tpu_custom_call" | custom-call | tf_op jit(solution)/shard_map/analysis/analysis/pallas_call | solution.py:423
Async XLA Ops:
  0.6 36.6 %copy-start.1 = (s32[1280]{0:T(1024)S(1)}, s32[1280]{0:T(1024)}, u32[]{:S(2)}) copy-start(s32[1280]{0:T(1024)} %order_ref.3) | copy-start | bytes 15364
  2.4 49.7 %copy-start = (s32[1,256]{1,0:T(1,128)S(1)}, s32[1,256]{1,0:T(1,128)}, u32[]{:S(2)}) copy-start(s32[1,256]{1,0:T(1,128)} %get-tuple-element.9) | copy-start | bytes 3076
  2.4 26.1 %all-to-all-start = ((f32[32,8,128]{2,1,0:T(8,128)}), f32[32,8,128]{2,1,0:T(8,128)S(1)}, u32[]{:S(2)}, u32[]{:S(2)}) async-start(f32[32,8,128]{2,1,0:T(8,128)} %bitcast.27), calls=%async_computation | async-start | bytes 262144 | tf_op jit(solution)/shard_map/all_to_all | solution.py:358
  28.5 23.6 %all-to-all-start.1 = ((bf16[256,4,128]{2,1,0:T(4,128)(2,1)}), bf16[256,4,128]{2,1,0:T(4,128)(2,1)}, u32[]{:S(2)}, u32[]{:S(2)}) async-start(bf16[256,4,128]{2,1,0:T(4,128)(2,1)} %bitcast.25), calls=%async_computation.1 | async-start | bytes 524288 | tf_op jit(solution)/shard_map/all_to_all | solution.py:385

commit v3 on v2

--- a/solution.py
+++ b/solution.py
@@ -130,9 +130,9 @@
     for half in range(2):
         rows = half_ref[half].astype(BF16)
         rows = jnp.concatenate([rows, rows], axis=0)
-        picked = [
-            lax.dot_general(row_picks(half, j), rows, NT, preferred_element_type=F32) for j in range(ROWS)
-        ]
+        picks = jnp.concatenate([row_picks(half, j) for j in range(ROWS)], axis=0)
+        picked = lax.dot_general(picks, rows, NT, preferred_element_type=F32)
+        picked = [picked[128 * j : 128 * j + 128] for j in range(ROWS)]
         picked.append(jnp.zeros_like(picked[0]))
         for jj in range(3):
             rows_ref[pl.ds(half * 512 + jj, 128, stride=4), :] = jnp.where(low, picked[2 * jj], picked[2 * jj + 1])
@@ -189,7 +189,7 @@
 
 def middle_kernel(
     place_smem, order_ref, obs_ref, rows_ref, phase_ref, inc_ref, out_ref,
-    wide_ref, turned_ref, grouped_ref, lhs_ref, grid_ref, acc_ref, seen_ref, table_ref, hot_ref,
+    wide_ref, turned_ref, grouped_ref, lhs_ref, grid_ref, acc_refs, seen_ref, table_ref, hot_ref, inc_buf, inc_sem,
 ):
     wide_ref[...] = rows_ref[...].astype(F32)
     for jj in range(3):
@@ -217,8 +217,11 @@
             grid_ref[pl.ds((a * 5 + u) * 64, 32), :] = pair
             grid_ref[pl.ds((a * 5 + u) * 64 + 32, 32), :] = pltpu.roll(pair, BLKW, 1)
         for j in range(ROWS):
-            inc_ref[j, :, pl.ds(QUARTER * a, QUARTER)] = rounded[6 * j : 6 * j + 6].astype(BF16)
-    acc_ref[...] = jnp.zeros_like(acc_ref)
+            inc_buf[j, :, pl.ds(QUARTER * a, QUARTER)] = rounded[6 * j : 6 * j + 6].astype(BF16)
+    inc_copy = pltpu.make_async_copy(inc_buf, inc_ref, inc_sem)
+    inc_copy.start()
+    for one in acc_refs:
+        one[...] = jnp.zeros_like(one)
     across = lanes((BLKW, 128), 0).astype(F32)
     pair_code = lanes((64, 128), 0).astype(F32)
     slot_code = (lanes((1, 128), 1) // KOBS * 8).astype(F32)
@@ -241,7 +244,7 @@
         back = (table_ref[d] * seen_ref[pl.ds(d, 1), :]).astype(BF16)
         spreads = lax.dot_general(hot_ref[d], back, NT, preferred_element_type=F32)
         for t in range(CAP):
-            acc_ref[pl.ds(place_smem[d * CAP + t], 8), pl.ds(0, BLKW)] += spreads[8 * t : 8 * t + 8]
+            acc_refs[t % 4][pl.ds(place_smem[d * CAP + t], 8), pl.ds(0, BLKW)] += spreads[8 * t : 8 * t + 8]
 
     def in_groups(step):
         def group(k, carry):
@@ -259,7 +262,9 @@
     low = lanes((32, 128), 1) < BLKW
 
     def pair_of(u):
-        return jnp.where(low, acc_ref[pl.ds(u * 64, 32), :], pltpu.roll(acc_ref[pl.ds(u * 64 + 32, 32), :], BLKW, 1))
+        left = sum(one[pl.ds(u * 64, 32), :] for one in acc_refs)
+        right = sum(one[pl.ds(u * 64 + 32, 32), :] for one in acc_refs)
+        return jnp.where(low, left, pltpu.roll(right, BLKW, 1))
 
     grads = [
         jnp.concatenate([pair_of(a * 5 + u) for u in range(5)], axis=1).astype(BF16).astype(F32) for a in range(4)
@@ -281,6 +286,7 @@
     for o in range(DEVS // N_LAT):
         wide_ref[pl.ds(4 * N_LAT * o + 3, N_LAT, stride=4), :] = seen_ref[...]
     out_ref[...] = wide_ref[...].astype(BF16)
+    inc_copy.wait()
 
 
 def analysis_kernel(
@@ -401,17 +407,19 @@
             middle_kernel,
             out_shape=(shape((ROWS, VARS, NLON), BF16), shape((4 * DEVS, 128), BF16)),
             in_specs=[SMEM, VMEM, VMEM, VMEM, VMEM],
-            out_specs=(VMEM, VMEM),
+            out_specs=(HBM, VMEM),
             scratch_shapes=[
                 pltpu.VMEM((4 * DEVS, 128), F32),
                 pltpu.VMEM((384, DEVS), F32),
                 pltpu.VMEM((2 * ORDERS, 32, DEVS), F32),
                 pltpu.VMEM((128, 2 * ORDERS * DEVS), BF16),
                 pltpu.VMEM((2 * CHUNKS * 32, 128), F32),
-                pltpu.VMEM((2 * CHUNKS * 32, 128), F32),
+                [pltpu.VMEM((2 * CHUNKS * 32, 128), F32)] * 4,
                 pltpu.VMEM((N_LAT, 128), F32),
                 pltpu.VMEM((N_LAT, BLKW, 128), F32),
                 pltpu.VMEM((N_LAT, 64, 128), BF16),
+                pltpu.VMEM((ROWS, VARS, NLON), BF16),
+                pltpu.SemaphoreType.DMA,
             ],
             compiler_params=grant(28),
             name="middle",

time: 86.7 us -> 86 us (level)
  transfers between devices with their start and end apart: 2 -> 2, of which waited for: 2 -> 2; matrix products, arithmetic and copies ran while one was open for 0% -> 0% of each run, Pallas kernels for 10% -> 9%
where the time goes in v3:
time: 86 us; the launch traced here: 85.6 us
  starting transfers between devices  23.3 us (27%)
  Pallas kernels  21.7 us (25%)
  blocking collectives  21.5 us (25%)
  waiting for transfers between devices  18 us (21%)
  between operations  0.86 us (1%)
    all_to_all x1, blocking collectives, shards(): lax.all_to_all(returning.reshape(DEVS, 4, 128), ('order', 'lat'), split_a...  21.5 us
    all_to_all x1, starting transfers between devices, shards(): lax.all_to_all(packed.reshape(N_LAT, 8, 128), 'lat', split_axis=0, concat...  14.6 us
    all_to_all x1, waiting for transfers between devices, shards(): lax.all_to_all(outgoing.reshape(DEVS, 4, 128), ('order', 'lat'), split_ax...  12.2 us
    all_to_all x1, starting transfers between devices, shards(): lax.all_to_all(outgoing.reshape(DEVS, 4, 128), ('order', 'lat'), split_ax...  8.67 us
    pallas_call x1, Pallas kernels, shards(): pl.pallas_call(analysis_kernel, out_shape=(shape((N_LAT, 128), F32), shap...  6.84 us
    all_to_all x1, waiting for transfers between devices, shards(): lax.all_to_all(packed.reshape(N_LAT, 8, 128), 'lat', split_axis=0, concat...  5.87 us
    pallas_call x1, Pallas kernels, shards(): pl.pallas_call(synth_kernel, out_shape=shape((4 * DEVS, 128), BF16), in_s...  5.64 us
    pallas_call x1, Pallas kernels, shards(): pl.pallas_call(middle_kernel, out_shape=(shape((ROWS, VARS, NLON), BF16),...  5 us
  transfers between devices with their start and end apart: 2, of which 2 were waited for; matrix products, arithmetic and copies ran while one was open for 0% of the time, Pallas kernels for 9%

profile of v3, /device:TPU:1, one launch (start us, length us, event | category | flops | bytes accessed | tf_op | source)
XLA Modules:
  0.0 85.6 jit_solution(3119507089741378815)
XLA Ops:
  0.6 0.0 copy-start.1
  0.6 1.7 %pack_obs.1 = (f32[256,128]{1,0:T(8,128)}, s32[1,256]{1,0:T(1,128)}) custom-call(s32[32,128]{1,0:T(8,128)} %bitcast.29, s32[32,128]{1,0:T(8,128)} %bitcast.30, f32[4,32,128]{2,1,0:T(8,128)} %bitcast.28, f32[32,128]{1,0:T(8,128)} %bitcast.31, f32[32,128]{1,0:T(8,128)} %bitcast.32, s32[1,32]{1,0:T(1,128)} %bitcast.35, s32[1,256]{1,0:T(1,128)} %bitcast.33, ...), custom_call_target="tpu_custom_call" | custom-call | tf_op jit(solution)/shard_map/pack_obs/pack_obs/pallas_call | solution.py:353
  2.4 0.0 copy-start
  2.4 14.6 %all-to-all-start = ((f32[32,8,128]{2,1,0:T(8,128)}), f32[32,8,128]{2,1,0:T(8,128)S(1)}, u32[]{:S(2)}, u32[]{:S(2)}) async-start(f32[32,8,128]{2,1,0:T(8,128)} %bitcast.27), calls=%async_computation | async-start | bytes 262144 | tf_op jit(solution)/shard_map/all_to_all | solution.py:364
  17.0 5.6 %synthesis.1 = bf16[1024,128]{1,0:T(8,128)(2,1)} custom-call(s32[1280]{0:T(1024)} %order_ref.3, f32[3,2,2,1280]{3,2,1,0:T(2,128)} %vertical_ref.3, f32[2,3,5,2,1280]{4,3,2,1,0:T(2,128)} %bitcast.23, bf16[5,1280,640]{2,1,0:T(8,128)(2,1)} %legendre_ref.3), custom_call_target="tpu_custom_call" | custom-call | flops 196608000 | bytes 9437184 | tf_op jit(solution)/shard_map/synthesis/synthesis/pallas_call | solution.py:373
  22.6 5.9 %all-to-all-done = f32[32,8,128]{2,1,0:T(8,128)S(1)} async-done(((f32[32,8,128]{2,1,0:T(8,128)}), f32[32,8,128]{2,1,0:T(8,128)S(1)}, u32[]{:S(2)}, u32[]{:S(2)}) %all-to-all-start) | async-done | bytes 131104 | tf_op jit(solution)/shard_map/all_to_all | solution.py:364
  28.5 8.7 %all-to-all-start.1 = ((bf16[256,4,128]{2,1,0:T(4,128)(2,1)}), bf16[256,4,128]{2,1,0:T(4,128)(2,1)}, u32[]{:S(2)}, u32[]{:S(2)}) async-start(bf16[256,4,128]{2,1,0:T(4,128)(2,1)} %bitcast.25), calls=%async_computation.1 | async-start | bytes 524288 | tf_op jit(solution)/shard_map/all_to_all | solution.py:391
  37.2 0.0 copy-done.1
  37.2 0.2 reshape.66.order_ref
  37.4 0.1 copy.16
  37.5 2.5 %phases.1.phase_ref = bf16[2560,640]{1,0:T(8,128)(2,1)S(1)} custom-call(s32[256,5]{1,0:T(8,128)S(1)} %reshape.66.order_ref), custom_call_target="tpu_custom_call" | custom-call | flops 40000000 | bytes 4194304 | tf_op jit(solution)/shard_map/phases/phases/pallas_call | solution.py:396
  39.9 12.2 %all-to-all-done.1 = bf16[256,4,128]{2,1,0:T(4,128)(2,1)} async-done(((bf16[256,4,128]{2,1,0:T(4,128)(2,1)}), bf16[256,4,128]{2,1,0:T(4,128)(2,1)}, u32[]{:S(2)}, u32[]{:S(2)}) %all-to-all-start.1) | async-done | bytes 262176 | tf_op jit(solution)/shard_map/all_to_all | solution.py:391
  52.1 0.0 copy-done
  52.1 5.0 %middle.1 = (bf16[5,6,2560]{2,1,0:T(8,128)(2,1)}, bf16[1024,128]{1,0:T(8,128)(2,1)S(1)}) custom-call(s32[256]{0:T(256)S(1)} %bitcast.22, s32[5,256]{1,0:T(8,128)S(1)} %bitcast.21, f32[256,128]{1,0:T(8,128)S(1)} %bitcast.19, bf16[1024,128]{1,0:T(8,128)(2,1)} %bitcast.14.rows_ref, bf16[2560,640]{1,0:T(8,128)(2,1)S(1)} %phases.1.phase_ref), custom_call_target="tpu_custom_call" | custom-call | tf_op jit(solution)/shard_map/middle/middle/pallas_call | solution.py:406
  57.1 21.5 %all_to_all.15 = bf16[256,4,128]{2,1,0:T(4,128)(2,1)} all-to-all(bf16[256,4,128]{2,1,0:T(4,128)(2,1)S(1)} %bitcast.20), channel_id=1, replica_groups=mesh['order'=8,'lat'=32] {'order','lat'}, dimensions={0} | all-to-all | bytes 524288 | tf_op jit(solution)/shard_map/all_to_all | solution.py:427
  78.6 6.8 %analysis.1 = (f32[32,128]{1,0:T(8,128)}, f32[2,3,5,2,1280]{4,3,2,1,0:T(2,128)}) custom-call(s32[1280]{0:T(1024)} %order_ref.3, f32[3,2,2,1280]{3,2,1,0:T(2,128)} %vertical_ref.3, f32[2,3,5,2,1280]{4,3,2,1,0:T(2,128)} %bitcast.24, bf16[5,1280,640]{2,1,0:T(8,128)(2,1)} %legendre_ref.3, bf16[1024,128]{1,0:T(8,128)(2,1)} %bitcast.26), custom_call_target="tpu_custom_call" | custom-call | tf_op jit(solution)/shard_map/analysis/analysis/pallas_call | solution.py:431
Async XLA Ops:
  0.6 36.6 %copy-start.1 = (s32[1280]{0:T(1024)S(1)}, s32[1280]{0:T(1024)}, u32[]{:S(2)}) copy-start(s32[1280]{0:T(1024)} %order_ref.3) | copy-start | bytes 15364
  2.4 49.7 %copy-start = (s32[1,256]{1,0:T(1,128)S(1)}, s32[1,256]{1,0:T(1,128)}, u32[]{:S(2)}) copy-start(s32[1,256]{1,0:T(1,128)} %get-tuple-element.9) | copy-start | bytes 3076
  2.4 26.1 %all-to-all-start = ((f32[32,8,128]{2,1,0:T(8,128)}), f32[32,8,128]{2,1,0:T(8,128)S(1)}, u32[]{:S(2)}, u32[]{:S(2)}) async-start(f32[32,8,128]{2,1,0:T(8,128)} %bitcast.27), calls=%async_computation | async-start | bytes 262144 | tf_op jit(solution)/shard_map/all_to_all | solution.py:364
  28.5 23.6 %all-to-all-start.1 = ((bf16[256,4,128]{2,1,0:T(4,128)(2,1)}), bf16[256,4,128]{2,1,0:T(4,128)(2,1)}, u32[]{:S(2)}, u32[]{:S(2)}) async-start(bf16[256,4,128]{2,1,0:T(4,128)(2,1)} %bitcast.25), calls=%async_computation.1 | async-start | bytes 524288 | tf_op jit(solution)/shard_map/all_to_all | solution.py:391

commit v4 on v3

--- a/solution.py
+++ b/solution.py
@@ -296,8 +296,11 @@
     small = start_small(order_ref, vertical_ref, control_ref, order_smem, vertical_buf, control_buf, small_sems)
     copies = start_tables(legendre_ref, table_ref, sems)
     wide_ref[...] = rows_ref[...].astype(F32)
-    first = lax.axis_index("order") * (4 * N_LAT)
-    weighted_ref[...] = wide_ref[pl.ds(first + 3, N_LAT, stride=4), :]
+    weighted = wide_ref[pl.ds(3, N_LAT, stride=4), :]
+    for o in range(1, DEVS // N_LAT):
+        mine = lax.axis_index("order") == o
+        weighted = jnp.where(mine, wide_ref[pl.ds(4 * N_LAT * o + 3, N_LAT, stride=4), :], weighted)
+    weighted_ref[...] = weighted
     for jj in range(3):
         turned_ref[pl.ds(128 * jj, 128), :] = wide_ref[pl.ds(jj, DEVS, stride=4), :].T
     for half in range(2):

time: 86 us -> 86 us (level)
  no operation moved by 1% of the time
where the time goes in v4:
time: 86 us; the launch traced here: 85.7 us
  starting transfers between devices  23.3 us (27%)
  Pallas kernels  21.7 us (25%)
  blocking collectives  21.5 us (25%)
  waiting for transfers between devices  18 us (21%)
  between operations  0.86 us (1%)
    all_to_all x1, blocking collectives, shards(): lax.all_to_all(returning.reshape(DEVS, 4, 128), ('order', 'lat'), split_a...  21.5 us
    all_to_all x1, starting transfers between devices, shards(): lax.all_to_all(packed.reshape(N_LAT, 8, 128), 'lat', split_axis=0, concat...  14.6 us
    all_to_all x1, waiting for transfers between devices, shards(): lax.all_to_all(outgoing.reshape(DEVS, 4, 128), ('order', 'lat'), split_ax...  12.2 us
    all_to_all x1, starting transfers between devices, shards(): lax.all_to_all(outgoing.reshape(DEVS, 4, 128), ('order', 'lat'), split_ax...  8.67 us
    pallas_call x1, Pallas kernels, shards(): pl.pallas_call(analysis_kernel, out_shape=(shape((N_LAT, 128), F32), shap...  6.88 us
    all_to_all x1, waiting for transfers between devices, shards(): lax.all_to_all(packed.reshape(N_LAT, 8, 128), 'lat', split_axis=0, concat...  5.87 us
    pallas_call x1, Pallas kernels, shards(): pl.pallas_call(synth_kernel, out_shape=shape((4 * DEVS, 128), BF16), in_s...  5.64 us
    pallas_call x1, Pallas kernels, shards(): pl.pallas_call(middle_kernel, out_shape=(shape((ROWS, VARS, NLON), BF16),...  5 us
  transfers between devices with their start and end apart: 2, of which 2 were waited for; matrix products, arithmetic and copies ran while one was open for 0% of the time, Pallas kernels for 9%

profile of v4, /device:TPU:1, one launch (start us, length us, event | category | flops | bytes accessed | tf_op | source)
XLA Modules:
  0.0 85.7 jit_solution(14393913608491938583)
XLA Ops:
  0.6 0.0 copy-start.1
  0.6 1.7 %pack_obs.1 = (f32[256,128]{1,0:T(8,128)}, s32[1,256]{1,0:T(1,128)}) custom-call(s32[32,128]{1,0:T(8,128)} %bitcast.29, s32[32,128]{1,0:T(8,128)} %bitcast.30, f32[4,32,128]{2,1,0:T(8,128)} %bitcast.28, f32[32,128]{1,0:T(8,128)} %bitcast.31, f32[32,128]{1,0:T(8,128)} %bitcast.32, s32[1,32]{1,0:T(1,128)} %bitcast.35, s32[1,256]{1,0:T(1,128)} %bitcast.33, ...), custom_call_target="tpu_custom_call" | custom-call | tf_op jit(solution)/shard_map/pack_obs/pack_obs/pallas_call | solution.py:356
  2.4 0.0 copy-start
  2.4 14.6 %all-to-all-start = ((f32[32,8,128]{2,1,0:T(8,128)}), f32[32,8,128]{2,1,0:T(8,128)S(1)}, u32[]{:S(2)}, u32[]{:S(2)}) async-start(f32[32,8,128]{2,1,0:T(8,128)} %bitcast.27), calls=%async_computation | async-start | bytes 262144 | tf_op jit(solution)/shard_map/all_to_all | solution.py:367
  17.0 5.6 %synthesis.1 = bf16[1024,128]{1,0:T(8,128)(2,1)} custom-call(s32[1280]{0:T(1024)} %order_ref.3, f32[3,2,2,1280]{3,2,1,0:T(2,128)} %vertical_ref.3, f32[2,3,5,2,1280]{4,3,2,1,0:T(2,128)} %bitcast.23, bf16[5,1280,640]{2,1,0:T(8,128)(2,1)} %legendre_ref.3), custom_call_target="tpu_custom_call" | custom-call | flops 196608000 | bytes 9437184 | tf_op jit(solution)/shard_map/synthesis/synthesis/pallas_call | solution.py:376
  22.6 5.9 %all-to-all-done = f32[32,8,128]{2,1,0:T(8,128)S(1)} async-done(((f32[32,8,128]{2,1,0:T(8,128)}), f32[32,8,128]{2,1,0:T(8,128)S(1)}, u32[]{:S(2)}, u32[]{:S(2)}) %all-to-all-start) | async-done | bytes 131104 | tf_op jit(solution)/shard_map/all_to_all | solution.py:367
  28.5 8.7 %all-to-all-start.1 = ((bf16[256,4,128]{2,1,0:T(4,128)(2,1)}), bf16[256,4,128]{2,1,0:T(4,128)(2,1)}, u32[]{:S(2)}, u32[]{:S(2)}) async-start(bf16[256,4,128]{2,1,0:T(4,128)(2,1)} %bitcast.25), calls=%async_computation.1 | async-start | bytes 524288 | tf_op jit(solution)/shard_map/all_to_all | solution.py:394
  37.2 0.0 copy-done.1
  37.2 0.2 reshape.66.order_ref
  37.4 0.1 copy.16
  37.5 2.5 %phases.1.phase_ref = bf16[2560,640]{1,0:T(8,128)(2,1)S(1)} custom-call(s32[256,5]{1,0:T(8,128)S(1)} %reshape.66.order_ref), custom_call_target="tpu_custom_call" | custom-call | flops 40000000 | bytes 4194304 | tf_op jit(solution)/shard_map/phases/phases/pallas_call | solution.py:399
  39.9 12.2 %all-to-all-done.1 = bf16[256,4,128]{2,1,0:T(4,128)(2,1)} async-done(((bf16[256,4,128]{2,1,0:T(4,128)(2,1)}), bf16[256,4,128]{2,1,0:T(4,128)(2,1)}, u32[]{:S(2)}, u32[]{:S(2)}) %all-to-all-start.1) | async-done | bytes 262176 | tf_op jit(solution)/shard_map/all_to_all | solution.py:394
  52.1 0.0 copy-done
  52.1 5.0 %middle.1 = (bf16[5,6,2560]{2,1,0:T(8,128)(2,1)}, bf16[1024,128]{1,0:T(8,128)(2,1)S(1)}) custom-call(s32[256]{0:T(256)S(1)} %bitcast.22, s32[5,256]{1,0:T(8,128)S(1)} %bitcast.21, f32[256,128]{1,0:T(8,128)S(1)} %bitcast.19, bf16[1024,128]{1,0:T(8,128)(2,1)} %bitcast.14.rows_ref, bf16[2560,640]{1,0:T(8,128)(2,1)S(1)} %phases.1.phase_ref), custom_call_target="tpu_custom_call" | custom-call | tf_op jit(solution)/shard_map/middle/middle/pallas_call | solution.py:409
  57.1 21.5 %all_to_all.15 = bf16[256,4,128]{2,1,0:T(4,128)(2,1)} all-to-all(bf16[256,4,128]{2,1,0:T(4,128)(2,1)S(1)} %bitcast.20), channel_id=1, replica_groups=mesh['order'=8,'lat'=32] {'order','lat'}, dimensions={0} | all-to-all | bytes 524288 | tf_op jit(solution)/shard_map/all_to_all | solution.py:430
  78.7 6.9 %analysis.1 = (f32[32,128]{1,0:T(8,128)}, f32[2,3,5,2,1280]{4,3,2,1,0:T(2,128)}) custom-call(s32[1280]{0:T(1024)} %order_ref.3, f32[3,2,2,1280]{3,2,1,0:T(2,128)} %vertical_ref.3, f32[2,3,5,2,1280]{4,3,2,1,0:T(2,128)} %bitcast.24, bf16[5,1280,640]{2,1,0:T(8,128)(2,1)} %legendre_ref.3, bf16[1024,128]{1,0:T(8,128)(2,1)} %bitcast.26), custom_call_target="tpu_custom_call" | custom-call | tf_op jit(solution)/shard_map/analysis/analysis/pallas_call | solution.py:434
Async XLA Ops:
  0.6 36.6 %copy-start.1 = (s32[1280]{0:T(1024)S(1)}, s32[1280]{0:T(1024)}, u32[]{:S(2)}) copy-start(s32[1280]{0:T(1024)} %order_ref.3) | copy-start | bytes 15364
  2.4 49.7 %copy-start = (s32[1,256]{1,0:T(1,128)S(1)}, s32[1,256]{1,0:T(1,128)}, u32[]{:S(2)}) copy-start(s32[1,256]{1,0:T(1,128)} %get-tuple-element.9) | copy-start | bytes 3076
  2.4 26.1 %all-to-all-start = ((f32[32,8,128]{2,1,0:T(8,128)}), f32[32,8,128]{2,1,0:T(8,128)S(1)}, u32[]{:S(2)}, u32[]{:S(2)}) async-start(f32[32,8,128]{2,1,0:T(8,128)} %bitcast.27), calls=%async_computation | async-start | bytes 262144 | tf_op jit(solution)/shard_map/all_to_all | solution.py:367
  28.5 23.6 %all-to-all-start.1 = ((bf16[256,4,128]{2,1,0:T(4,128)(2,1)}), bf16[256,4,128]{2,1,0:T(4,128)(2,1)}, u32[]{:S(2)}, u32[]{:S(2)}) async-start(bf16[256,4,128]{2,1,0:T(4,128)(2,1)} %bitcast.25), calls=%async_computation.1 | async-start | bytes 524288 | tf_op jit(solution)/shard_map/all_to_all | solution.py:394
